TPU v7x, 128 devices: a whole 4x4x4 slice. The times are simulated.
128 devices in a mesh: dp: 32 (over z, y, core), ctx: 4 (over x).
Axes of the slice: x: 4, y: 4, z: 4, core: 2. Of those that a mesh axis runs over, the one named last changes fastest.
Arguments:
- queries: bfloat16 [90112, 2048], P(('dp', 'ctx')), may hold values from -8 to 8
- keys: bfloat16 [90112, 512], P(('dp', 'ctx')), may hold values from -8 to 8
- values: bfloat16 [90112, 512], P(('dp', 'ctx')), may hold values from -6 to 6
- out_grad: bfloat16 [90112, 2048], P(('dp', 'ctx')), may hold values from -6 to 6
- short_lengths: int32 [128, 4], P(('dp', 'ctx')), may hold values from 1 to 64, 128 in all within a row
- doc_lengths: int32 [64], replicated, may hold values from 0 to 2304, as said below
- doc_group: int32 [64], replicated, may hold values from 0 to 31
- doc_offset: int32 [64], replicated, may hold values from 0 to 2304, as said below
Outputs:
- attended: bfloat16 [90112, 2048], P(('dp', 'ctx'))
- query_grads: bfloat16 [90112, 2048], P(('dp', 'ctx'))
- key_grads: bfloat16 [90112, 512], P(('dp', 'ctx'))
- value_grads: bfloat16 [90112, 512], P(('dp', 'ctx'))
Inputs may be any that keep to these rules, and one draw needn't show every extreme that they name: `short_lengths`: each row sums to 128. `doc_lengths`: each group is named by exactly 2 documents; the nonempty documents of a group tile its positions 0 to 4 * 576 - 1 without gaps; every length is 0 or a multiple of 4 * 32 and at least 8 times that. `doc_offset`: an empty document has offset 4 * 576.
All inputs are finite; a program needn't handle non-finite values.
Results may differ from a plain program's by a relative error of at most 0.0054.
The roundings to bfloat16 on the way count: a program that leaves them out, or rounds other values in their place, can miss the bound.
Values may be sent and summed in bfloat16 or wider, within the bound.
A program may use at most 192 MiB of HBM per device.

v0:
```python
import math

import jax
import jax.numpy as jnp
from jax import lax
from jax.sharding import PartitionSpec as P

HQ = 16
HK = 4
DH = 128
SHORT_DEV = 128
LONG_DEV = 576


MASKED = -1e30


def for_sending(shard):
    return jax.tree.map(lambda a: a.astype(jnp.bfloat16) if a.dtype == jnp.float32 else a, shard)


def short_segments(lengths, count):
    ends = jnp.cumsum(lengths, dtype=jnp.int32)
    positions = jnp.arange(count, dtype=jnp.int32)
    return jnp.sum((positions[:, None] >= ends[None, :]).astype(jnp.int32), axis=1, dtype=jnp.int32)


def doc_segments(positions, group_id, doc_lengths, doc_group, doc_offset):
    inside = (
        (doc_group[None, :] == group_id)
        & (positions[:, None] >= doc_offset[None, :])
        & (positions[:, None] < doc_offset[None, :] + doc_lengths[None, :])
    )
    labels = jnp.arange(1, doc_lengths.shape[0] + 1, dtype=jnp.int32)
    return jnp.sum(jnp.where(inside, labels[None, :], 0), axis=1, dtype=jnp.int32)


def head_split(blocks):
    count, rows, _ = blocks.shape
    return blocks.reshape(count, rows, HK, HQ // HK, DH).transpose(2, 0, 1, 3, 4)


def head_join(parts):
    heads, count, rows, group, size = parts.shape
    return parts.transpose(1, 2, 0, 3, 4).reshape(count, rows, heads * group * size)


def key_split(blocks):
    count, rows, _ = blocks.shape
    return blocks.reshape(count, rows, HK, DH).transpose(2, 0, 1, 3)


def key_join(parts):
    heads, count, rows, size = parts.shape
    return parts.transpose(1, 2, 0, 3).reshape(count, rows, heads * size)


def stat_split(blocks):
    count, rows, _ = blocks.shape
    return blocks.reshape(count, rows, HK, HQ // HK).transpose(2, 0, 3, 1)


def stat_join(parts):
    heads, count, group, rows = parts.shape
    return parts.transpose(1, 3, 0, 2).reshape(count, rows, heads * group)


def collect(pick, parts):
    shaped = pick.reshape(pick.shape + (1,) * (parts.ndim - 1))
    return jnp.sum(jnp.where(shaped, parts[None], 0.0), axis=1)


def tile_mask(query_pos, query_seg, key_pos, key_seg, tile_q, tile_k):
    row_pos = query_pos[tile_q]
    row_seg = query_seg[tile_q]
    col_pos = key_pos[tile_k]
    col_seg = key_seg[tile_k]
    return (row_seg[:, :, None] == col_seg[:, None, :]) & (
        col_pos[:, None, :] <= row_pos[:, :, None]
    )


def tile_scores(tile_query, tile_key, allowed):
    scaling = 1.0 / math.sqrt(DH)
    scores = (
        jnp.einsum("tqgd,tkd->tgqk", tile_query, tile_key, preferred_element_type=jnp.float32)
        * scaling
    )
    return jnp.where(allowed[:, None], scores, MASKED)


def forward_tiles(query_blocks, key_blocks, value_blocks, tile_q, tile_k, allowed):
    query_count = query_blocks.shape[0]
    pick = tile_q[None, :] == jnp.arange(query_count, dtype=jnp.int32)[:, None]

    def forward_one_head(operands):
        head_query, head_key, head_value = operands
        scores = tile_scores(head_query[tile_q], head_key[tile_k], allowed)
        tile_max = jnp.max(scores, axis=3)
        block_max = jnp.max(jnp.where(pick[:, :, None, None], tile_max[None], MASKED), axis=1)
        shifted = jnp.exp(scores - block_max[tile_q][..., None])
        block_sum = collect(pick, jnp.sum(shifted, axis=3))
        log_total = block_max + jnp.log(block_sum)
        weights = jnp.exp(scores - log_total[tile_q][..., None]).astype(jnp.bfloat16)
        part = jnp.einsum(
            "tgqk,tkd->tqgd", weights, head_value[tile_k], preferred_element_type=jnp.float32
        )
        return (collect(pick, part).astype(jnp.bfloat16), log_total)

    outputs, totals = lax.map(
        forward_one_head, (head_split(query_blocks), key_split(key_blocks), key_split(value_blocks))
    )
    return (head_join(outputs), stat_join(totals))


def backward_tiles(
    query_blocks,
    grad_blocks,
    total_blocks,
    product_blocks,
    key_blocks,
    value_blocks,
    tile_q,
    tile_k,
    allowed,
):
    query_count = query_blocks.shape[0]
    key_count = key_blocks.shape[0]
    scaling = 1.0 / math.sqrt(DH)
    query_pick = tile_q[None, :] == jnp.arange(query_count, dtype=jnp.int32)[:, None]
    key_pick = tile_k[None, :] == jnp.arange(key_count, dtype=jnp.int32)[:, None]

    def backward_one_head(operands):
        head_query, head_grad, head_total, head_product, head_key, head_value = operands
        tile_query = head_query[tile_q]
        tile_grad = head_grad[tile_q]
        tile_key = head_key[tile_k]
        scores = tile_scores(tile_query, tile_key, allowed)
        weights_full = jnp.exp(scores - head_total[tile_q][..., None])
        weight_grads = jnp.einsum(
            "tqgd,tkd->tgqk", tile_grad, head_value[tile_k], preferred_element_type=jnp.float32
        )
        score_grads = (weights_full * (weight_grads - head_product[tile_q][..., None])).astype(
            jnp.bfloat16
        )
        results = []
        query_part = (
            jnp.einsum("tgqk,tkd->tqgd", score_grads, tile_key, preferred_element_type=jnp.float32)
            * scaling
        )
        results.append(collect(query_pick, query_part))
        weights = weights_full.astype(jnp.bfloat16)
        value_part = jnp.einsum(
            "tgqk,tqgd->tkd", weights, tile_grad, preferred_element_type=jnp.float32
        )
        key_part = (
            jnp.einsum(
                "tgqk,tqgd->tkd", score_grads, tile_query, preferred_element_type=jnp.float32
            )
            * scaling
        )
        results.append(collect(key_pick, key_part))
        results.append(collect(key_pick, value_part))
        return tuple(results)

    results = lax.map(
        backward_one_head,
        (
            head_split(query_blocks),
            head_split(grad_blocks),
            stat_split(total_blocks),
            stat_split(product_blocks),
            key_split(key_blocks),
            key_split(value_blocks),
        ),
    )
    joined_results = []
    index = 0
    joined_results.append(head_join(results[index]))
    index = index + 1
    joined_results.append(key_join(results[index]))
    joined_results.append(key_join(results[index + 1]))
    return tuple(joined_results)


def row_products(grad_rows, out_rows):
    row_count = grad_rows.shape[0]
    joint = grad_rows.astype(jnp.float32) * out_rows.astype(jnp.float32)
    return jnp.sum(joint.reshape(row_count, HQ, DH), axis=2)


def per_device(queries, keys, values, out_grad, short_lengths, doc_lengths, doc_group, doc_offset):
    groups = lax.axis_size("dp")
    members = lax.axis_size("ctx")
    group_id = lax.axis_index("dp")
    member = lax.axis_index("ctx")
    group_span = members * LONG_DEV
    half = LONG_DEV // 2

    def pieces(row_array):
        return row_array.reshape(groups, row_array.shape[0] // groups, row_array.shape[1])

    def joined(piece_array):
        return piece_array.reshape(LONG_DEV, piece_array.shape[2])

    def blocks(row_array):
        return row_array.reshape(row_array.shape[0] // half, half, row_array.shape[1])

    long_query, long_key, long_value, long_grad = (
        lax.all_to_all(pieces(queries[SHORT_DEV:]), "dp", split_axis=0, concat_axis=0, tiled=True),
        lax.all_to_all(pieces(keys[SHORT_DEV:]), "dp", split_axis=0, concat_axis=0, tiled=True),
        lax.all_to_all(pieces(values[SHORT_DEV:]), "dp", split_axis=0, concat_axis=0, tiled=True),
        lax.all_to_all(pieces(out_grad[SHORT_DEV:]), "dp", split_axis=0, concat_axis=0, tiled=True),
    )
    long_query = joined(long_query)
    long_key = joined(long_key)
    long_value = joined(long_value)
    long_grad = joined(long_grad)
    single = jnp.zeros((1,), jnp.int32)
    short_seg = short_segments(short_lengths[0], SHORT_DEV)[None]
    short_pos = jnp.arange(SHORT_DEV, dtype=jnp.int32)[None]
    short_allowed = tile_mask(short_pos, short_seg, short_pos, short_seg, single, single)
    short_query = queries[:SHORT_DEV][None]
    short_key = keys[:SHORT_DEV][None]
    short_value = values[:SHORT_DEV][None]
    short_grad = out_grad[:SHORT_DEV][None]
    short_out, short_totals = forward_tiles(
        short_query, short_key, short_value, single, single, short_allowed
    )
    short_products = row_products(short_grad[0], short_out[0])[None]
    short_dq, short_dk, short_dv = backward_tiles(
        short_query,
        short_grad,
        short_totals,
        short_products,
        short_key,
        short_value,
        single,
        single,
        short_allowed,
    )
    whole_key, whole_value = (
        lax.all_gather(long_key, "ctx", axis=0, tiled=True),
        lax.all_gather(long_value, "ctx", axis=0, tiled=True),
    )
    segments = doc_segments(
        jnp.arange(group_span, dtype=jnp.int32), group_id, doc_lengths, doc_group, doc_offset
    )
    member_ids = jnp.arange(members, dtype=jnp.int32)
    starts = jnp.stack([member_ids * half, (2 * members - 1 - member_ids) * half], axis=1).reshape(
        2 * members
    )
    block_pos = starts[:, None] + jnp.arange(half, dtype=jnp.int32)[None, :]
    block_seg = segments[block_pos]
    own_pos = lax.dynamic_slice_in_dim(block_pos, 2 * member, 2, 0)
    own_seg = lax.dynamic_slice_in_dim(block_seg, 2 * member, 2, 0)
    steps_ids = jnp.arange(members + 1, dtype=jnp.int32)
    earlier = steps_ids <= member
    tile_q = jnp.concatenate(
        [jnp.ones((members,), jnp.int32), jnp.where(earlier, 0, 1).astype(jnp.int32)]
    )
    tile_k = jnp.concatenate([2 * member_ids, jnp.where(earlier, 2 * steps_ids, 2 * steps_ids - 1)])
    long_allowed = tile_mask(own_pos, own_seg, block_pos, block_seg, tile_q, tile_k)
    query_blocks = blocks(long_query)
    grad_blocks = blocks(long_grad)
    out_blocks, total_blocks = forward_tiles(
        query_blocks, blocks(whole_key), blocks(whole_value), tile_q, tile_k, long_allowed
    )
    long_out = out_blocks.reshape(LONG_DEV, out_blocks.shape[2])
    long_products = row_products(long_grad, long_out)
    product_blocks = blocks(long_products)
    dq_blocks, partial_dk, partial_dv = backward_tiles(
        query_blocks,
        grad_blocks,
        total_blocks,
        product_blocks,
        blocks(whole_key),
        blocks(whole_value),
        tile_q,
        tile_k,
        long_allowed,
    )
    long_dk, long_dv = (
        lax.psum_scatter(
            partial_dk.reshape(group_span, partial_dk.shape[2]),
            "ctx",
            scatter_dimension=0,
            tiled=True,
        ),
        lax.psum_scatter(
            partial_dv.reshape(group_span, partial_dv.shape[2]),
            "ctx",
            scatter_dimension=0,
            tiled=True,
        ),
    )
    long_dq = dq_blocks.reshape(LONG_DEV, dq_blocks.shape[2]).astype(jnp.bfloat16)
    long_dk = long_dk.astype(jnp.bfloat16)
    long_dv = long_dv.astype(jnp.bfloat16)
    back_out, back_dq, back_dk, back_dv = (
        lax.all_to_all(
            for_sending(pieces(long_out)), "dp", split_axis=0, concat_axis=0, tiled=True
        ),
        lax.all_to_all(for_sending(pieces(long_dq)), "dp", split_axis=0, concat_axis=0, tiled=True),
        lax.all_to_all(for_sending(pieces(long_dk)), "dp", split_axis=0, concat_axis=0, tiled=True),
        lax.all_to_all(for_sending(pieces(long_dv)), "dp", split_axis=0, concat_axis=0, tiled=True),
    )
    attended = jnp.concatenate([short_out[0], joined(back_out)], axis=0)
    query_grads = jnp.concatenate([short_dq[0].astype(jnp.bfloat16), joined(back_dq)], axis=0)
    key_grads = jnp.concatenate([short_dk[0].astype(jnp.bfloat16), joined(back_dk)], axis=0)
    value_grads = jnp.concatenate([short_dv[0].astype(jnp.bfloat16), joined(back_dv)], axis=0)
    return (attended, query_grads, key_grads, value_grads)


def solution(mesh):
    in_specs = (
        P(("dp", "ctx"), None),
        P(("dp", "ctx"), None),
        P(("dp", "ctx"), None),
        P(("dp", "ctx"), None),
        P(("dp", "ctx"), None),
        P(),
        P(),
        P(),
    )
    out_specs = (
        P(("dp", "ctx"), None),
        P(("dp", "ctx"), None),
        P(("dp", "ctx"), None),
        P(("dp", "ctx"), None),
    )
    return jax.shard_map(
        per_device, mesh=mesh, in_specs=in_specs, out_specs=out_specs, check_vma=False
    )
```

profile of v0, /device:TPU:1, one launch (start us, length us, event | category | flops | bytes accessed | tf_op | source)
XLA Modules:
  0.0 754.1 jit_solution(14578377501872145793)
XLA Ops:
  8.6 23.6 %all_to_all.40 = bf16[32,18,512]{2,1,0:T(8,128)(2,1)S(1)} all-to-all(bf16[32,18,512]{2,1,0:T(8,128)(2,1)S(1)} %reshape.556), channel_id=1, replica_groups=mesh['dp'=32,'ctx'=4] {'dp'}, dimensions={0} | all-to-all | bytes 1179648 | tf_op jit(solution)/shard_map/all_to_all | solution.py:212
  34.3 4.1 all-to-all-start.1
  40.9 11.9 %all-to-all-done.1 = bf16[32,18,512]{2,1,0:T(8,128)(2,1)S(1)} async-done(((bf16[32,18,512]{2,1,0:T(8,128)(2,1)}), bf16[32,18,512]{2,1,0:T(8,128)(2,1)S(1)}, u32[]{:S(2)}, u32[]{:S(2)}) %all-to-all-start.1) | async-done | bytes 589856 | tf_op jit(solution)/shard_map/all_to_all | solution.py:211
  53.6 4.3 all-to-all-start.2
  60.3 3.4 slice.31
  63.7 4.3 reshape.563
  68.0 29.2 %all-to-all-done.2 = bf16[32,18,2048]{2,1,0:T(8,128)(2,1)S(1)} async-done(((bf16[32,18,2048]{2,1,0:T(8,128)(2,1)}), bf16[32,18,2048]{2,1,0:T(8,128)(2,1)S(1)}, u32[]{:S(2)}, u32[]{:S(2)}) %all-to-all-start.2) | async-done | bytes 2359328 | tf_op jit(solution)/shard_map/all_to_all | solution.py:210
  98.8 6.6 all-to-all-start.4
  106.0 12.3 %gather_fusion.11 = s32[2304]{0:T(1024)S(1)} fusion(s32[2304]{0:T(1024)S(1)} %select_reduce_fusion.6, s32[3072]{0:T(1024)S(1)} %pad_clamp_fusion.4), kind=kCustom, calls=%fused_computation.11 | custom fusion | bytes 27648 | tf_op jit(solution)/shard_map/gather | solution.py:254
  121.1 6.4 reshape_reshape_reshape.10
  127.5 3.7 copy.149
  131.2 13.5 %all-to-all-done.4 = bf16[32,18,2048]{2,1,0:T(8,128)(2,1)S(1)} async-done(((bf16[32,18,2048]{2,1,0:T(8,128)(2,1)}), bf16[32,18,2048]{2,1,0:T(8,128)(2,1)S(1)}, u32[]{:S(2)}, u32[]{:S(2)}) %all-to-all-start.4) | async-done | bytes 2359328 | tf_op jit(solution)/shard_map/all_to_all | solution.py:213
  144.7 3.0 reshape.617
  150.4 4.2 reshape_reshape.19
  156.3 4.2 reshape_reshape.20
  162.3 154.2 %while.60 = (s32[]{:T(128)}, bf16[4,2,288,4,128]{4,2,3,1,0:T(8,128)(2,1)}, f32[4,2,4,288]{3,2,1,0:T(4,128)}, bf16[4,8,288,128]{3,2,1,0:T(8,128)(2,1)}, s32[9]{0:...) while((s32[]{:T(128)}, ...), condition=%wide.region_13.14_spmd.clone.clone, body=%wide.region_7.13_spmd.clone.clone.sunk | while | flops 1568984576 | bytes 75542736 | solution.py:110
  169.7 8.8 %fusion.188 = (f32[9,4,288]{2,1,0:T(4,128)S(1)}, f32[9,288,288,4]{2,1,3,0:T(8,128)}) fusion(pred[9,288,288]{1,2,0:T(8,128)(4,1)S(1)} %compare_and_fusion.4, bf16[9,288,4,128]{3,1,2,0:T(8,128)(2,1)S(1)} %gather_fusion, bf16[9,288,128]{2,1,0:T(8,128)(2,1)} %gather_fusion.1), kind=kOutput, calls=%fused_computation.96.clone.1 | convolution fusion | flops 773359488 | bytes 16049664 | tf_op jit(solution)/shard_map/while/body/eval_jaxpr/tqgd,tkd->tgqk/dot_general | solution.py:86
  179.2 9.8 %exponential_reduce_fusion.5 = f32[9,4,288]{2,1,0:T(4,128)S(1)} fusion(f32[9,288,288,4]{2,1,3,0:T(8,128)} %get-tuple-element.1030, f32[9,4,288]{2,1,0:T(4,128)S(1)} %gather_fusion.2, pred[9,288,288]{1,2,0:T(8,128)(4,1)} %copy-done.2), kind=kLoop, calls=%fused_computation.95.clone.1 | loop fusion | flops 11933568 | bytes 12773376 | tf_op jit(solution)/shard_map/while/body/eval_jaxpr/reduce_sum | solution.py:102
  191.1 8.2 %fusion.189 = f32[9,288,4,128]{3,1,2,0:T(8,128)S(1)} fusion(f32[9,288,288,4]{2,1,3,0:T(8,128)} %get-tuple-element.1030, f32[9,4,288]{2,1,0:T(4,128)S(1)} %gather_fusion.3, pred[9,288,288]{1,2,0:T(8,128)(4,1)S(1)} %copy-done.3, bf16[9,288,128]{2,1,0:T(8,128)(2,1)S(1)} %gather_fusion.4), kind=kOutput, calls=%fused_computation.104.clone.1 | convolution fusion | flops 776355840 | bytes 18703872 | tf_op jit(solution)/shard_map/while/body/eval_jaxpr/tgqk,tkd->tqgd/dot_general | solution.py:105
  208.2 8.8 %fusion.188 = (f32[9,4,288]{2,1,0:T(4,128)S(1)}, f32[9,288,288,4]{2,1,3,0:T(8,128)}) fusion(pred[9,288,288]{1,2,0:T(8,128)(4,1)S(1)} %compare_and_fusion.4, bf16[9,288,4,128]{3,1,2,0:T(8,128)(2,1)S(1)} %gather_fusion, bf16[9,288,128]{2,1,0:T(8,128)(2,1)} %gather_fusion.1), kind=kOutput, calls=%fused_computation.96.clone.1 | convolution fusion | flops 773359488 | bytes 16049664 | tf_op jit(solution)/shard_map/while/body/eval_jaxpr/tqgd,tkd->tgqk/dot_general | solution.py:86
  217.7 9.8 %exponential_reduce_fusion.5 = f32[9,4,288]{2,1,0:T(4,128)S(1)} fusion(f32[9,288,288,4]{2,1,3,0:T(8,128)} %get-tuple-element.1030, f32[9,4,288]{2,1,0:T(4,128)S(1)} %gather_fusion.2, pred[9,288,288]{1,2,0:T(8,128)(4,1)} %copy-done.2), kind=kLoop, calls=%fused_computation.95.clone.1 | loop fusion | flops 11933568 | bytes 12773376 | tf_op jit(solution)/shard_map/while/body/eval_jaxpr/reduce_sum | solution.py:102
  229.6 8.2 %fusion.189 = f32[9,288,4,128]{3,1,2,0:T(8,128)S(1)} fusion(f32[9,288,288,4]{2,1,3,0:T(8,128)} %get-tuple-element.1030, f32[9,4,288]{2,1,0:T(4,128)S(1)} %gather_fusion.3, pred[9,288,288]{1,2,0:T(8,128)(4,1)S(1)} %copy-done.3, bf16[9,288,128]{2,1,0:T(8,128)(2,1)S(1)} %gather_fusion.4), kind=kOutput, calls=%fused_computation.104.clone.1 | convolution fusion | flops 776355840 | bytes 18703872 | tf_op jit(solution)/shard_map/while/body/eval_jaxpr/tgqk,tkd->tqgd/dot_general | solution.py:105
  246.6 8.8 %fusion.188 = (f32[9,4,288]{2,1,0:T(4,128)S(1)}, f32[9,288,288,4]{2,1,3,0:T(8,128)}) fusion(pred[9,288,288]{1,2,0:T(8,128)(4,1)S(1)} %compare_and_fusion.4, bf16[9,288,4,128]{3,1,2,0:T(8,128)(2,1)S(1)} %gather_fusion, bf16[9,288,128]{2,1,0:T(8,128)(2,1)} %gather_fusion.1), kind=kOutput, calls=%fused_computation.96.clone.1 | convolution fusion | flops 773359488 | bytes 16049664 | tf_op jit(solution)/shard_map/while/body/eval_jaxpr/tqgd,tkd->tgqk/dot_general | solution.py:86
  256.1 9.8 %exponential_reduce_fusion.5 = f32[9,4,288]{2,1,0:T(4,128)S(1)} fusion(f32[9,288,288,4]{2,1,3,0:T(8,128)} %get-tuple-element.1030, f32[9,4,288]{2,1,0:T(4,128)S(1)} %gather_fusion.2, pred[9,288,288]{1,2,0:T(8,128)(4,1)} %copy-done.2), kind=kLoop, calls=%fused_computation.95.clone.1 | loop fusion | flops 11933568 | bytes 12773376 | tf_op jit(solution)/shard_map/while/body/eval_jaxpr/reduce_sum | solution.py:102
  268.0 8.2 %fusion.189 = f32[9,288,4,128]{3,1,2,0:T(8,128)S(1)} fusion(f32[9,288,288,4]{2,1,3,0:T(8,128)} %get-tuple-element.1030, f32[9,4,288]{2,1,0:T(4,128)S(1)} %gather_fusion.3, pred[9,288,288]{1,2,0:T(8,128)(4,1)S(1)} %copy-done.3, bf16[9,288,128]{2,1,0:T(8,128)(2,1)S(1)} %gather_fusion.4), kind=kOutput, calls=%fused_computation.104.clone.1 | convolution fusion | flops 776355840 | bytes 18703872 | tf_op jit(solution)/shard_map/while/body/eval_jaxpr/tgqk,tkd->tqgd/dot_general | solution.py:105
  285.0 8.8 %fusion.188 = (f32[9,4,288]{2,1,0:T(4,128)S(1)}, f32[9,288,288,4]{2,1,3,0:T(8,128)}) fusion(pred[9,288,288]{1,2,0:T(8,128)(4,1)S(1)} %compare_and_fusion.4, bf16[9,288,4,128]{3,1,2,0:T(8,128)(2,1)S(1)} %gather_fusion, bf16[9,288,128]{2,1,0:T(8,128)(2,1)} %gather_fusion.1), kind=kOutput, calls=%fused_computation.96.clone.1 | convolution fusion | flops 773359488 | bytes 16049664 | tf_op jit(solution)/shard_map/while/body/eval_jaxpr/tqgd,tkd->tgqk/dot_general | solution.py:86
  294.6 9.8 %exponential_reduce_fusion.5 = f32[9,4,288]{2,1,0:T(4,128)S(1)} fusion(f32[9,288,288,4]{2,1,3,0:T(8,128)} %get-tuple-element.1030, f32[9,4,288]{2,1,0:T(4,128)S(1)} %gather_fusion.2, pred[9,288,288]{1,2,0:T(8,128)(4,1)} %copy-done.2), kind=kLoop, calls=%fused_computation.95.clone.1 | loop fusion | flops 11933568 | bytes 12773376 | tf_op jit(solution)/shard_map/while/body/eval_jaxpr/reduce_sum | solution.py:102
  306.5 8.2 %fusion.189 = f32[9,288,4,128]{3,1,2,0:T(8,128)S(1)} fusion(f32[9,288,288,4]{2,1,3,0:T(8,128)} %get-tuple-element.1030, f32[9,4,288]{2,1,0:T(4,128)S(1)} %gather_fusion.3, pred[9,288,288]{1,2,0:T(8,128)(4,1)S(1)} %copy-done.3, bf16[9,288,128]{2,1,0:T(8,128)(2,1)S(1)} %gather_fusion.4), kind=kOutput, calls=%fused_computation.104.clone.1 | convolution fusion | flops 776355840 | bytes 18703872 | tf_op jit(solution)/shard_map/while/body/eval_jaxpr/tgqk,tkd->tqgd/dot_general | solution.py:105
  318.9 5.1 fusion.104
  324.2 246.4 %while.61 = (s32[]{:T(128)}, bf16[4,2,288,4,128]{4,2,3,1,0:T(8,128)(2,1)}, f32[4,8,288,128]{3,2,1,0:T(8,128)}, f32[4,8,288,128]{3,2,1,0:T(8,128)}, bf16[4,8,288,...) while((s32[]{:T(128)}, ...), condition=%wide.region_22.23_spmd.clone.clone, body=%wide.region_18.22_spmd.clone.clone.sunk | while | flops 3870860288 | bytes 145116112 | solution.py:166
  342.8 7.8 %fusion.202 = f32[9,288,288,4]{2,1,3,0:T(8,128)} fusion(bf16[9,288,4,128]{3,1,2,0:T(8,128)(2,1)S(1)} %gather_fusion.5, bf16[9,288,128]{2,1,0:T(8,128)(2,1)S(1)} %gather_fusion.6), kind=kOutput, calls=%fused_computation.147.clone.1 | convolution fusion | flops 764411904 | bytes 15261696 | tf_op jit(solution)/shard_map/while/body/eval_jaxpr/tqgd,tkd->tgqk/dot_general | solution.py:86
  360.3 11.7 %fusion.203 = bf16[9,4,288,288]{2,3,1,0:T(8,128)(2,1)} fusion(f32[9,288,288,4]{2,1,3,0:T(8,128)} %fusion.202, bf16[9,288,4,128]{3,1,2,0:T(8,128)(2,1)} %gather_fusion.7, f32[9,4,288]{2,1,0:T(4,128)S(1)} %gather_fusion.8, f32[9,4,288]{2,1,0:T(4,128)S(1)} %gather_fusion.9, pred[9,288,288]{1,2,0:T(8,128)(4,1)S(1)} %compare_and_fusion.5, ...), kind=kOutput, calls=%fused_computation.127.clone.1 | convolution fusion | flops 782327808 | bytes 22063104 | tf_op jit(solution)/shard_map/while/body/eval_jaxpr/tqgd,tkd->tgqk/dot_general | solution.py:140
  372.0 5.0 fusion.205
  377.1 9.1 %fusion.204 = f32[9,288,128]{2,1,0:T(8,128)S(1)} fusion(bf16[9,288,4,128]{3,1,2,0:T(8,128)(2,1)} %gather_fusion.7, f32[9,288,288,4]{2,1,3,0:T(8,128)} %fusion.202, f32[9,4,288]{2,1,0:T(4,128)S(1)} %gather_fusion.9, pred[9,288,288]{1,2,0:T(8,128)(4,1)} %copy-done.6), kind=kOutput, calls=%fused_computation.139.clone.1 | convolution fusion | flops 776355840 | bytes 16713216 | tf_op jit(solution)/shard_map/while/body/eval_jaxpr/tgqk,tqgd->tkd/dot_general | solution.py:153
  390.5 3.0 multiply_bitcast_fusion.3
  401.2 7.8 %fusion.202 = f32[9,288,288,4]{2,1,3,0:T(8,128)} fusion(bf16[9,288,4,128]{3,1,2,0:T(8,128)(2,1)S(1)} %gather_fusion.5, bf16[9,288,128]{2,1,0:T(8,128)(2,1)S(1)} %gather_fusion.6), kind=kOutput, calls=%fused_computation.147.clone.1 | convolution fusion | flops 764411904 | bytes 15261696 | tf_op jit(solution)/shard_map/while/body/eval_jaxpr/tqgd,tkd->tgqk/dot_general | solution.py:86
  418.6 11.7 %fusion.203 = bf16[9,4,288,288]{2,3,1,0:T(8,128)(2,1)} fusion(f32[9,288,288,4]{2,1,3,0:T(8,128)} %fusion.202, bf16[9,288,4,128]{3,1,2,0:T(8,128)(2,1)} %gather_fusion.7, f32[9,4,288]{2,1,0:T(4,128)S(1)} %gather_fusion.8, f32[9,4,288]{2,1,0:T(4,128)S(1)} %gather_fusion.9, pred[9,288,288]{1,2,0:T(8,128)(4,1)S(1)} %compare_and_fusion.5, ...), kind=kOutput, calls=%fused_computation.127.clone.1 | convolution fusion | flops 782327808 | bytes 22063104 | tf_op jit(solution)/shard_map/while/body/eval_jaxpr/tqgd,tkd->tgqk/dot_general | solution.py:140
  430.4 5.0 fusion.205
  435.4 9.1 %fusion.204 = f32[9,288,128]{2,1,0:T(8,128)S(1)} fusion(bf16[9,288,4,128]{3,1,2,0:T(8,128)(2,1)} %gather_fusion.7, f32[9,288,288,4]{2,1,3,0:T(8,128)} %fusion.202, f32[9,4,288]{2,1,0:T(4,128)S(1)} %gather_fusion.9, pred[9,288,288]{1,2,0:T(8,128)(4,1)} %copy-done.6), kind=kOutput, calls=%fused_computation.139.clone.1 | convolution fusion | flops 776355840 | bytes 16713216 | tf_op jit(solution)/shard_map/while/body/eval_jaxpr/tgqk,tqgd->tkd/dot_general | solution.py:153
  448.9 3.0 multiply_bitcast_fusion.3
  459.6 7.8 %fusion.202 = f32[9,288,288,4]{2,1,3,0:T(8,128)} fusion(bf16[9,288,4,128]{3,1,2,0:T(8,128)(2,1)S(1)} %gather_fusion.5, bf16[9,288,128]{2,1,0:T(8,128)(2,1)S(1)} %gather_fusion.6), kind=kOutput, calls=%fused_computation.147.clone.1 | convolution fusion | flops 764411904 | bytes 15261696 | tf_op jit(solution)/shard_map/while/body/eval_jaxpr/tqgd,tkd->tgqk/dot_general | solution.py:86
  477.0 11.7 %fusion.203 = bf16[9,4,288,288]{2,3,1,0:T(8,128)(2,1)} fusion(f32[9,288,288,4]{2,1,3,0:T(8,128)} %fusion.202, bf16[9,288,4,128]{3,1,2,0:T(8,128)(2,1)} %gather_fusion.7, f32[9,4,288]{2,1,0:T(4,128)S(1)} %gather_fusion.8, f32[9,4,288]{2,1,0:T(4,128)S(1)} %gather_fusion.9, pred[9,288,288]{1,2,0:T(8,128)(4,1)S(1)} %compare_and_fusion.5, ...), kind=kOutput, calls=%fused_computation.127.clone.1 | convolution fusion | flops 782327808 | bytes 22063104 | tf_op jit(solution)/shard_map/while/body/eval_jaxpr/tqgd,tkd->tgqk/dot_general | solution.py:140
  488.7 5.0 fusion.205
  493.8 9.1 %fusion.204 = f32[9,288,128]{2,1,0:T(8,128)S(1)} fusion(bf16[9,288,4,128]{3,1,2,0:T(8,128)(2,1)} %gather_fusion.7, f32[9,288,288,4]{2,1,3,0:T(8,128)} %fusion.202, f32[9,4,288]{2,1,0:T(4,128)S(1)} %gather_fusion.9, pred[9,288,288]{1,2,0:T(8,128)(4,1)} %copy-done.6), kind=kOutput, calls=%fused_computation.139.clone.1 | convolution fusion | flops 776355840 | bytes 16713216 | tf_op jit(solution)/shard_map/while/body/eval_jaxpr/tgqk,tqgd->tkd/dot_general | solution.py:153
  507.2 3.0 multiply_bitcast_fusion.3
  517.9 7.8 %fusion.202 = f32[9,288,288,4]{2,1,3,0:T(8,128)} fusion(bf16[9,288,4,128]{3,1,2,0:T(8,128)(2,1)S(1)} %gather_fusion.5, bf16[9,288,128]{2,1,0:T(8,128)(2,1)S(1)} %gather_fusion.6), kind=kOutput, calls=%fused_computation.147.clone.1 | convolution fusion | flops 764411904 | bytes 15261696 | tf_op jit(solution)/shard_map/while/body/eval_jaxpr/tqgd,tkd->tgqk/dot_general | solution.py:86
  535.3 11.7 %fusion.203 = bf16[9,4,288,288]{2,3,1,0:T(8,128)(2,1)} fusion(f32[9,288,288,4]{2,1,3,0:T(8,128)} %fusion.202, bf16[9,288,4,128]{3,1,2,0:T(8,128)(2,1)} %gather_fusion.7, f32[9,4,288]{2,1,0:T(4,128)S(1)} %gather_fusion.8, f32[9,4,288]{2,1,0:T(4,128)S(1)} %gather_fusion.9, pred[9,288,288]{1,2,0:T(8,128)(4,1)S(1)} %compare_and_fusion.5, ...), kind=kOutput, calls=%fused_computation.127.clone.1 | convolution fusion | flops 782327808 | bytes 22063104 | tf_op jit(solution)/shard_map/while/body/eval_jaxpr/tqgd,tkd->tgqk/dot_general | solution.py:140
  547.0 5.0 fusion.205
  552.1 9.1 %fusion.204 = f32[9,288,128]{2,1,0:T(8,128)S(1)} fusion(bf16[9,288,4,128]{3,1,2,0:T(8,128)(2,1)} %gather_fusion.7, f32[9,288,288,4]{2,1,3,0:T(8,128)} %fusion.202, f32[9,4,288]{2,1,0:T(4,128)S(1)} %gather_fusion.9, pred[9,288,288]{1,2,0:T(8,128)(4,1)} %copy-done.6), kind=kOutput, calls=%fused_computation.139.clone.1 | convolution fusion | flops 776355840 | bytes 16713216 | tf_op jit(solution)/shard_map/while/body/eval_jaxpr/tgqk,tqgd->tkd/dot_general | solution.py:153
  565.5 3.0 multiply_bitcast_fusion.3
  570.6 5.4 copy.168
  584.5 6.7 all-to-all-start.5
  597.9 5.4 copy.170
  608.6 5.5 reshape_reshape_reshape.11
  614.1 16.4 %all-to-all-done.5 = bf16[32,18,2048]{2,1,0:T(8,128)(2,1)S(1)} async-done(((bf16[32,18,2048]{2,1,0:T(8,128)(2,1)}), bf16[32,18,2048]{2,1,0:T(8,128)(2,1)S(1)}, u32[]{:S(2)}, u32[]{:S(2)}) %all-to-all-start.5) | async-done | bytes 2359328 | tf_op jit(solution)/shard_map/all_to_all | solution.py:304
  630.5 7.3 all-to-all-start.3
  637.8 8.7 %while.58 = (s32[]{:T(128)}, bf16[4,1,128,4,128]{2,4,3,1,0:T(8,128)(2,1)}, f32[4,1,4,128]{3,2,1,0:T(4,128)S(1)}, bf16[4,1,128,128]{2,3,1,0:T(8,128)(2,1)S(1)}, b...) while((s32[]{:T(128)}, ...), condition=%wide.region_5.6_spmd.clone, body=%wide.region_2.5_spmd.clone.sunk | while | flops 34127360 | bytes 1165913 | solution.py:110
  663.0 14.1 %all-to-all-done.3 = bf16[32,18,2048]{2,1,0:T(8,128)(2,1)} async-done(((bf16[32,18,2048]{2,1,0:T(8,128)(2,1)}), bf16[32,18,2048]{2,1,0:T(8,128)(2,1)}, u32[]{:S(2)}, u32[]{:S(2)}) %all-to-all-start.3) | async-done | bytes 2359328 | tf_op jit(solution)/shard_map/all_to_all | solution.py:301
  677.1 7.1 all-to-all-start.6
  684.2 26.5 %while.59 = (s32[]{:T(128)}, bf16[4,1,128,4,128]{2,4,3,1,0:T(8,128)(2,1)}, bf16[4,1,128,128]{3,2,1,0:T(8,128)(2,1)}, bf16[4,1,128,128]{3,2,1,0:T(8,128)(2,1)}, b...) while((s32[]{:T(128)}, ...), condition=%wide.region_16.17_spmd.clone, body=%wide.region_15.16_spmd.clone.sunk | while | flops 84475904 | bytes 2246265 | solution.py:166
  714.7 4.3 reshape.561
  723.3 7.5 %all-to-all-start.7 = ((bf16[32,18,512]{2,1,0:T(8,128)(2,1)}), bf16[32,18,512]{2,1,0:T(8,128)(2,1)}, u32[]{:S(2)}, u32[]{:S(2)}) async-start(bf16[32,18,512]{2,1,0:T(8,128)(2,1)} %reshape.567), calls=%async_computation.9 | async-start | bytes 1572864 | tf_op jit(solution)/shard_map/all_to_all | solution.py:306
  730.9 3.7 pad_maximum_fusion
  736.8 3.7 pad_maximum_fusion.1
  (394 shorter events, 243.8 us)
Async XLA Ops:
  7.2 26.0 %slice-start.1 = ((bf16[704,512]{1,0:T(8,128)(2,1)}), bf16[576,512]{1,0:T(8,128)(2,1)S(1)}, s32[]{:S(2)}) async-start(bf16[704,512]{1,0:T(8,128)(2,1)} %param.17), calls=%async_computation.15 | async-start | bytes 1179648 | tf_op jit(solution)/shard_map/slice | solution.py:211
  7.2 143.2 %all-gather.3.cloned.1.call-start = ((), (), s32[]{:S(2)}) async-start(), calls=%async_computation.10 | async-start | bytes 2949120 | tf_op jit(solution)/shard_map/all_gather | solution.py:244
  33.2 5.2 slice-start
  34.3 18.5 %all-to-all-start.1 = ((bf16[32,18,512]{2,1,0:T(8,128)(2,1)}), bf16[32,18,512]{2,1,0:T(8,128)(2,1)S(1)}, u32[]{:S(2)}, u32[]{:S(2)}) async-start(bf16[32,18,512]{2,1,0:T(8,128)(2,1)} %reshape.558), calls=%async_computation.1 | async-start | bytes 1572864 | tf_op jit(solution)/shard_map/all_to_all | solution.py:211
  52.8 0.9 copy-start.9
  53.6 43.6 %all-to-all-start.2 = ((bf16[32,18,2048]{2,1,0:T(8,128)(2,1)}), bf16[32,18,2048]{2,1,0:T(8,128)(2,1)S(1)}, u32[]{:S(2)}, u32[]{:S(2)}) async-start(bf16[32,18,2048]{2,1,0:T(8,128)(2,1)} %reshape.560), calls=%async_computation.2 | async-start | bytes 6291456 | tf_op jit(solution)/shard_map/all_to_all | solution.py:210
  57.9 98.4 %all-gather.5.cloned.1.call-start = ((), (), s32[]{:S(2)}) async-start(), calls=%async_computation.11 | async-start | bytes 2949120 | tf_op jit(solution)/shard_map/all_gather | solution.py:243
  68.0 37.6 %copy-start.10 = (s32[64]{0:T(128)S(1)}, s32[64]{0:T(128)}, u32[]{:S(2)}) copy-start(s32[64]{0:T(128)} %param.23) | copy-start | bytes 772
  68.0 37.6 %copy-start.11 = (s32[64]{0:T(128)S(1)}, s32[64]{0:T(128)}, u32[]{:S(2)}) copy-start(s32[64]{0:T(128)} %param.21) | copy-start | bytes 772
  68.0 37.7 %copy-start.12 = (s32[64]{0:T(128)S(1)}, s32[64]{0:T(128)}, u32[]{:S(2)}) copy-start(s32[64]{0:T(128)} %param.22) | copy-start | bytes 772
  97.2 1.6 copy-start.7
  98.8 45.8 %all-to-all-start.4 = ((bf16[32,18,2048]{2,1,0:T(8,128)(2,1)}), bf16[32,18,2048]{2,1,0:T(8,128)(2,1)S(1)}, u32[]{:S(2)}, u32[]{:S(2)}) async-start(bf16[32,18,2048]{2,1,0:T(8,128)(2,1)} %reshape.563), calls=%async_computation.4 | async-start | bytes 6291456 | tf_op jit(solution)/shard_map/all_to_all | solution.py:213
  105.4 553.3 %reduce-scatter.3.cloned.1.call-start = ((), (), s32[]{:S(2)}) async-start(), calls=%async_computation.12 | async-start | bytes 5898240 | tf_op jit(solution)/shard_map/reduce_scatter | solution.py:284
  169.7 8.8 %copy-start.2 = (pred[9,288,288]{1,2,0:T(8,128)(4,1)}, pred[9,288,288]{1,2,0:T(8,128)(4,1)S(1)}, u32[]{:S(2)}) copy-start(pred[9,288,288]{1,2,0:T(8,128)(4,1)S(1)} %compare_and_fusion.4) | copy-start | bytes 2239492 | tf_op jit(solution)/shard_map/while
  179.2 11.2 %copy-start.5 = (bf16[8,288,128]{2,1,0:T(8,128)(2,1)S(1)}, bf16[8,288,128]{2,1,0:T(8,128)(2,1)}, u32[]{:S(2)}) copy-start(bf16[8,288,128]{2,1,0:T(8,128)(2,1)} %get-tuple-element.1033) | copy-start | bytes 1769476 | tf_op jit(solution)/shard_map/while
  179.2 11.9 %copy-start.3 = (pred[9,288,288]{1,2,0:T(8,128)(4,1)S(1)}, pred[9,288,288]{1,2,0:T(8,128)(4,1)}, u32[]{:S(2)}) copy-start(pred[9,288,288]{1,2,0:T(8,128)(4,1)} %copy-done.2) | copy-start | bytes 2239492 | tf_op jit(solution)/shard_map/while
  208.1 8.8 %copy-start.2 = (pred[9,288,288]{1,2,0:T(8,128)(4,1)}, pred[9,288,288]{1,2,0:T(8,128)(4,1)S(1)}, u32[]{:S(2)}) copy-start(pred[9,288,288]{1,2,0:T(8,128)(4,1)S(1)} %compare_and_fusion.4) | copy-start | bytes 2239492 | tf_op jit(solution)/shard_map/while
  217.7 11.2 %copy-start.5 = (bf16[8,288,128]{2,1,0:T(8,128)(2,1)S(1)}, bf16[8,288,128]{2,1,0:T(8,128)(2,1)}, u32[]{:S(2)}) copy-start(bf16[8,288,128]{2,1,0:T(8,128)(2,1)} %get-tuple-element.1033) | copy-start | bytes 1769476 | tf_op jit(solution)/shard_map/while
  217.7 11.9 %copy-start.3 = (pred[9,288,288]{1,2,0:T(8,128)(4,1)S(1)}, pred[9,288,288]{1,2,0:T(8,128)(4,1)}, u32[]{:S(2)}) copy-start(pred[9,288,288]{1,2,0:T(8,128)(4,1)} %copy-done.2) | copy-start | bytes 2239492 | tf_op jit(solution)/shard_map/while
  246.6 8.8 %copy-start.2 = (pred[9,288,288]{1,2,0:T(8,128)(4,1)}, pred[9,288,288]{1,2,0:T(8,128)(4,1)S(1)}, u32[]{:S(2)}) copy-start(pred[9,288,288]{1,2,0:T(8,128)(4,1)S(1)} %compare_and_fusion.4) | copy-start | bytes 2239492 | tf_op jit(solution)/shard_map/while
  256.1 11.2 %copy-start.5 = (bf16[8,288,128]{2,1,0:T(8,128)(2,1)S(1)}, bf16[8,288,128]{2,1,0:T(8,128)(2,1)}, u32[]{:S(2)}) copy-start(bf16[8,288,128]{2,1,0:T(8,128)(2,1)} %get-tuple-element.1033) | copy-start | bytes 1769476 | tf_op jit(solution)/shard_map/while
  256.1 11.9 %copy-start.3 = (pred[9,288,288]{1,2,0:T(8,128)(4,1)S(1)}, pred[9,288,288]{1,2,0:T(8,128)(4,1)}, u32[]{:S(2)}) copy-start(pred[9,288,288]{1,2,0:T(8,128)(4,1)} %copy-done.2) | copy-start | bytes 2239492 | tf_op jit(solution)/shard_map/while
  285.0 8.8 %copy-start.2 = (pred[9,288,288]{1,2,0:T(8,128)(4,1)}, pred[9,288,288]{1,2,0:T(8,128)(4,1)S(1)}, u32[]{:S(2)}) copy-start(pred[9,288,288]{1,2,0:T(8,128)(4,1)S(1)} %compare_and_fusion.4) | copy-start | bytes 2239492 | tf_op jit(solution)/shard_map/while
  294.6 11.2 %copy-start.5 = (bf16[8,288,128]{2,1,0:T(8,128)(2,1)S(1)}, bf16[8,288,128]{2,1,0:T(8,128)(2,1)}, u32[]{:S(2)}) copy-start(bf16[8,288,128]{2,1,0:T(8,128)(2,1)} %get-tuple-element.1033) | copy-start | bytes 1769476 | tf_op jit(solution)/shard_map/while
  294.6 11.9 %copy-start.3 = (pred[9,288,288]{1,2,0:T(8,128)(4,1)S(1)}, pred[9,288,288]{1,2,0:T(8,128)(4,1)}, u32[]{:S(2)}) copy-start(pred[9,288,288]{1,2,0:T(8,128)(4,1)} %copy-done.2) | copy-start | bytes 2239492 | tf_op jit(solution)/shard_map/while
  342.8 7.8 %copy-start = (bf16[9,288,128]{2,1,0:T(8,128)(2,1)}, bf16[9,288,128]{2,1,0:T(8,128)(2,1)S(1)}, u32[]{:S(2)}) copy-start(bf16[9,288,128]{2,1,0:T(8,128)(2,1)S(1)} %gather_fusion.6) | copy-start | bytes 1990660 | tf_op jit(solution)/shard_map/while
  360.3 11.8 %copy-start.6 = (pred[9,288,288]{1,2,0:T(8,128)(4,1)}, pred[9,288,288]{1,2,0:T(8,128)(4,1)S(1)}, u32[]{:S(2)}) copy-start(pred[9,288,288]{1,2,0:T(8,128)(4,1)S(1)} %compare_and_fusion.5) | copy-start | bytes 2239492 | tf_op jit(solution)/shard_map/while
  386.3 4.2 copy-start.1
  386.3 4.2 copy-start.4
  401.2 7.8 %copy-start = (bf16[9,288,128]{2,1,0:T(8,128)(2,1)}, bf16[9,288,128]{2,1,0:T(8,128)(2,1)S(1)}, u32[]{:S(2)}) copy-start(bf16[9,288,128]{2,1,0:T(8,128)(2,1)S(1)} %gather_fusion.6) | copy-start | bytes 1990660 | tf_op jit(solution)/shard_map/while
  418.6 11.8 %copy-start.6 = (pred[9,288,288]{1,2,0:T(8,128)(4,1)}, pred[9,288,288]{1,2,0:T(8,128)(4,1)S(1)}, u32[]{:S(2)}) copy-start(pred[9,288,288]{1,2,0:T(8,128)(4,1)S(1)} %compare_and_fusion.5) | copy-start | bytes 2239492 | tf_op jit(solution)/shard_map/while
  444.6 4.3 copy-start.1
  444.6 4.3 copy-start.4
  459.6 7.8 %copy-start = (bf16[9,288,128]{2,1,0:T(8,128)(2,1)}, bf16[9,288,128]{2,1,0:T(8,128)(2,1)S(1)}, u32[]{:S(2)}) copy-start(bf16[9,288,128]{2,1,0:T(8,128)(2,1)S(1)} %gather_fusion.6) | copy-start | bytes 1990660 | tf_op jit(solution)/shard_map/while
  477.0 11.8 %copy-start.6 = (pred[9,288,288]{1,2,0:T(8,128)(4,1)}, pred[9,288,288]{1,2,0:T(8,128)(4,1)S(1)}, u32[]{:S(2)}) copy-start(pred[9,288,288]{1,2,0:T(8,128)(4,1)S(1)} %compare_and_fusion.5) | copy-start | bytes 2239492 | tf_op jit(solution)/shard_map/while
  503.0 4.2 copy-start.1
  503.0 4.2 copy-start.4
  517.9 7.8 %copy-start = (bf16[9,288,128]{2,1,0:T(8,128)(2,1)}, bf16[9,288,128]{2,1,0:T(8,128)(2,1)S(1)}, u32[]{:S(2)}) copy-start(bf16[9,288,128]{2,1,0:T(8,128)(2,1)S(1)} %gather_fusion.6) | copy-start | bytes 1990660 | tf_op jit(solution)/shard_map/while
  535.3 11.7 %copy-start.6 = (pred[9,288,288]{1,2,0:T(8,128)(4,1)}, pred[9,288,288]{1,2,0:T(8,128)(4,1)S(1)}, u32[]{:S(2)}) copy-start(pred[9,288,288]{1,2,0:T(8,128)(4,1)S(1)} %compare_and_fusion.5) | copy-start | bytes 2239492 | tf_op jit(solution)/shard_map/while
  561.3 4.2 copy-start.1
  561.3 4.2 copy-start.4
  584.5 12.7 %slice-start.2 = ((bf16[704,512]{1,0:T(8,128)(2,1)}), bf16[128,512]{1,0:T(8,128)(2,1)S(1)}, s32[]{:S(2)}) async-start(bf16[704,512]{1,0:T(8,128)(2,1)} %param.17), calls=%async_computation.16 | async-start | bytes 262144 | tf_op jit(solution)/shard_map/slice | solution.py:224
  584.5 13.0 %slice-start.3 = ((bf16[704,512]{1,0:T(8,128)(2,1)}), bf16[128,512]{1,0:T(8,128)(2,1)S(1)}, s32[]{:S(2)}) async-start(bf16[704,512]{1,0:T(8,128)(2,1)} %param.18), calls=%async_computation.17 | async-start | bytes 262144 | tf_op jit(solution)/shard_map/slice | solution.py:225
  584.5 13.1 %copy-start.13 = (s32[1,4]{1,0:T(1,128)S(1)}, s32[1,4]{1,0:T(1,128)}, u32[]{:S(2)}) copy-start(s32[1,4]{1,0:T(1,128)} %param.20) | copy-start | bytes 52
  584.5 46.0 %all-to-all-start.5 = ((bf16[32,18,2048]{2,1,0:T(8,128)(2,1)}), bf16[32,18,2048]{2,1,0:T(8,128)(2,1)S(1)}, u32[]{:S(2)}, u32[]{:S(2)}) async-start(bf16[32,18,2048]{2,1,0:T(8,128)(2,1)} %convert_element_type.120), calls=%async_computation.5 | async-start | bytes 6291456 | tf_op jit(solution)/shard_map/all_to_all | solution.py:304
  591.2 127.8 %reduce-scatter.5.cloned.1.call-start = ((), (), s32[]{:S(2)}) async-start(), calls=%async_computation.13 | async-start | bytes 5898240 | tf_op jit(solution)/shard_map/reduce_scatter | solution.py:290
  603.3 2.7 copy-start.8
  630.5 46.6 %all-to-all-start.3 = ((bf16[32,18,2048]{2,1,0:T(8,128)(2,1)}), bf16[32,18,2048]{2,1,0:T(8,128)(2,1)}, u32[]{:S(2)}, u32[]{:S(2)}) async-start(bf16[32,18,2048]{2,1,0:T(8,128)(2,1)} %reshape_reshape_reshape.11), calls=%async_computation.3 | async-start | bytes 6291456 | tf_op jit(solution)/shard_map/all_to_all | solution.py:301
  677.1 46.2 %all-to-all-start.6 = ((bf16[32,18,512]{2,1,0:T(8,128)(2,1)}), bf16[32,18,512]{2,1,0:T(8,128)(2,1)}, u32[]{:S(2)}, u32[]{:S(2)}) async-start(bf16[32,18,512]{2,1,0:T(8,128)(2,1)} %reshape.565), calls=%async_computation.7 | async-start | bytes 1572864 | tf_op jit(solution)/shard_map/all_to_all | solution.py:305
  723.3 21.8 %all-to-all-start.7 = ((bf16[32,18,512]{2,1,0:T(8,128)(2,1)}), bf16[32,18,512]{2,1,0:T(8,128)(2,1)}, u32[]{:S(2)}, u32[]{:S(2)}) async-start(bf16[32,18,512]{2,1,0:T(8,128)(2,1)} %reshape.567), calls=%async_computation.9 | async-start | bytes 1572864 | tf_op jit(solution)/shard_map/all_to_all | solution.py:306
Sparse Core Ops, SparseCore 0:
  33.3 30.4 all-gather.2
  66.1 33.0 all-gather.4
  578.9 50.0 reduce-scatter.2
  631.2 50.7 reduce-scatter.4
where the time goes:
time: 765 us; the launch traced here: 754 us
  matrix products  249 us (33%)
  local copies, waits for them, and re-layouts  227 us (30%)
  other arithmetic  93.8 us (12%)
  waiting for transfers between devices  87.6 us (11%)
  starting transfers between devices  43.8 us (6%)
  blocking collectives  23.6 us (3%)
  loops' own time  14.9 us (2%)
  between operations  14.4 us (2%)
    dot_general x16, matrix products, tile_scores(): jnp.einsum('tqgd,tkd->tgqk', tile_query, tile_key, preferred_element_type...  75.2 us
    dot_general x8, matrix products, backward_one_head(): jnp.einsum('tqgd,tkd->tgqk', tile_grad, head_value[tile_k], preferred_ele...  51.4 us
    dot_general x8, matrix products, backward_one_head(): jnp.einsum('tgqk,tqgd->tkd', weights, tile_grad, preferred_element_type=j...  43.3 us
    reduce_sum x8, other arithmetic, forward_one_head(): block_sum = collect(pick, jnp.sum(shifted, axis=3))  39.6 us
    dot_general x8, matrix products, forward_one_head(): jnp.einsum('tgqk,tkd->tqgd', weights, head_value[tile_k], preferred_eleme...  36.4 us
    squeeze x20, local copies, waits for them, and re-layouts, forward_tiles(): lax.map(forward_one_head, (head_split(query_blocks), key_split(key_blocks...  29.5 us
    all_to_all x1, waiting for transfers between devices, per_device(): lax.all_to_all(pieces(queries[SHORT_DEV:]), 'dp', split_axis=0, concat_ax...  29.2 us
    dot_general x8, matrix products, backward_one_head(): jnp.einsum('tgqk,tqgd->tkd', score_grads, tile_query, preferred_element_t...  27 us
  transfers between devices with their start and end apart: 11, of which 6 were waited for; matrix products, arithmetic and copies ran while one was open for 21% of the time, Pallas kernels for 0%

commit v1 on v0

v1 whole, which is shorter than its diff:
```python
import functools
import math

import jax
import jax.numpy as jnp
from jax import lax
from jax.experimental import pallas as pl
from jax.experimental.pallas import tpu as pltpu
from jax.sharding import PartitionSpec as P

HQ = 16
HK = 4
DH = 128
SHORT_DEV = 128
LONG_DEV = 576
ROWS = SHORT_DEV + LONG_DEV

N_DEV = 128
GROUPS = 32
PIECE = LONG_DEV // GROUPS
SLAB = 8 * PIECE
SPAN = N_DEV * PIECE
PAIR = 2
TILE = 768
SUB = 256
ROWS_A = 112
ROWS_B = 72

SCALE = 1.0 / math.sqrt(DH)
SCALE2 = math.log2(math.e) / math.sqrt(DH)
MASKED = -1e30
FAR = 1 << 20
F32 = jnp.float32
BF16 = jnp.bfloat16
MESH = pl.DeviceIdType.MESH


def dot(a, b, dim_a, dim_b):
    return lax.dot_general(
        a, b, (((dim_a,), (dim_b,)), ((), ())), preferred_element_type=F32
    )


def by_eight(x):
    return x.reshape(x.shape[0] // 8, 8, x.shape[1])


def over_rows(x, op):
    return jnp.broadcast_to(op(x, axis=0, keepdims=True), (8, x.shape[1]))


def position_of(dp, ctx):
    return jnp.where(dp < 16, ctx * 16 + dp, (7 - ctx) * 16 + dp - 16)


TURNS = ((1, 0), (0, 1), (3, 0), (0, 3), (1, 3), (3, 1), (2, 2), (0, 2),
         (2, 0), (1, 1), (3, 3), (1, 2), (3, 2), (2, 1), (2, 3), (0, 0))


def each_partner(dp, ctx, body):
    def wrap(value, size):
        return jnp.where(value >= size, value - size, value)

    xs = [wrap(ctx + i, 4) for i in range(4)]
    ys = [wrap(lax.rem(dp // 2, 4) + i, 4) * 2 for i in range(4)]

    def turn(j, turns):
        z = wrap(dp // 8 + lax.rem(j, 4), 4)
        core = wrap(lax.rem(dp, 2) + j // 4, 2)
        zs = [wrap(z + i, 4) * 8 for i in range(4)]
        cores = [core, 1 - core]
        for x, y in turns:
            body(zs[(x + y) % 4] + ys[y] + cores[x % 2], xs[x])

    def step(j, carry):
        turn(j, TURNS)
        return carry

    turn(0, TURNS[:-1])
    lax.fori_loop(1, 8, step, 0)


def attend_tile(i, bound, q_ref, g_ref, k_ref, v_ref, kt_ref, vt_ref, o_ref, dq_ref,
                dk_acc, dv_acc, s_buf, o_acc, dq_acc):
    subs = TILE // SUB
    wide = PAIR * SUB
    total = PAIR * TILE
    start = pl.multiple_of(i * TILE, TILE)

    def at(a):
        return pl.ds(pl.multiple_of(start + a * SUB, SUB), SUB)

    def gather(ref):
        return jnp.concatenate([ref[h, at(a), :] for a in range(subs) for h in range(PAIR)], 0)

    q = gather(q_ref)
    g = gather(g_ref)
    row = start + jnp.concatenate(
        [lax.broadcasted_iota(jnp.int32, (8, SUB), 1) + a * SUB
         for a in range(subs) for _ in range(PAIR)], 1)

    def scores(k0, count, first, diagonal, maxima):
        lane0 = first * wide
        maxima = list(maxima)
        for t in range(0, count, 128):
            c0 = pl.multiple_of(k0 + t, 128)
            s = by_eight(dot(k_ref[pl.ds(c0, 128), :], q[lane0:], 1, 1))
            limit = jnp.where(c0 < bound, bound, FAR)
            s = s + jnp.where(row[:, lane0:] >= limit, MASKED, 0.0)[None]
            for a in range(first, subs):
                part = s[:, :, (a - first) * wide:(a - first + 1) * wide]
                if diagonal and a == first:
                    key = (lax.broadcasted_iota(jnp.int32, part.shape, 0) * 8
                           + lax.broadcasted_iota(jnp.int32, part.shape, 1) + c0)
                    part = jnp.where(key > row[None, :, a * wide:(a + 1) * wide], MASKED, part)
                s_buf[pl.ds(c0, 128), a * wide:(a + 1) * wide] = part.reshape(128, wide)
                maxima[a] = jnp.maximum(maxima[a], jnp.max(part, axis=0))
        return tuple(maxima)

    def sweep(body, carry):
        carry = lax.fori_loop(
            0, i, lambda kb, x: body(pl.multiple_of(kb * TILE, TILE), TILE, 0, False, x), carry)
        for a in range(subs):
            carry = body(pl.multiple_of(start + a * SUB, SUB), SUB, a, True, carry)
        return carry

    maxima = sweep(scores, tuple(jnp.full((8, wide), MASKED, F32) for _ in range(subs)))
    top = jnp.concatenate([over_rows(x, jnp.max) * SCALE2 for x in maxima], 1)

    def powers(k0, count, first, diagonal, sums):
        lane0 = first * wide
        p = jnp.exp2(by_eight(s_buf[pl.ds(k0, count), lane0:]) * SCALE2 - top[None, :, lane0:])
        s_buf[pl.ds(k0, count), lane0:] = p.reshape(count, total - lane0)
        added = jnp.sum(p, axis=0)
        return tuple(
            x if a < first else x + added[:, (a - first) * wide:(a - first + 1) * wide]
            for a, x in enumerate(sums))

    sums = sweep(powers, tuple(jnp.zeros((8, wide), F32) for _ in range(subs)))
    inverse = jnp.concatenate([1.0 / over_rows(x, jnp.sum) for x in sums], 1)

    o_acc[...] = jnp.zeros_like(o_acc)

    def outputs(k0, count, first, diagonal, carry):
        lane0 = first * wide
        w = by_eight(s_buf[pl.ds(k0, count), lane0:]) * inverse[None, :, lane0:]
        w = w.reshape(count, total - lane0).astype(BF16)
        o_acc[:, lane0:] += dot(vt_ref[:, pl.ds(k0, count)], w, 1, 0)
        dv_acc[pl.ds(k0, count), :] += dot(w, g[lane0:], 1, 0)
        return carry

    sweep(outputs, 0)
    out = o_acc[...].astype(BF16)

    def put(ref, x):
        x = x.T
        for a in range(subs):
            for h in range(PAIR):
                ref[h, at(a), :] = x[(a * PAIR + h) * SUB:(a * PAIR + h + 1) * SUB]

    put(o_ref, out)
    product = over_rows(g.T.astype(F32) * out.astype(F32), jnp.sum)
    dq_acc[...] = jnp.zeros_like(dq_acc)

    def backward(k0, count, first, diagonal, carry):
        lane0 = first * wide
        dp = by_eight(dot(v_ref[pl.ds(k0, count), :], g[lane0:], 1, 1))
        w = by_eight(s_buf[pl.ds(k0, count), lane0:]) * inverse[None, :, lane0:]
        ds = (w * (dp - product[None, :, lane0:])).reshape(count, total - lane0).astype(BF16)
        dq_acc[:, lane0:] += dot(kt_ref[:, pl.ds(k0, count)], ds, 1, 0)
        dk_acc[pl.ds(k0, count), :] += dot(ds, q[lane0:], 1, 0)
        return carry

    sweep(backward, 0)
    put(dq_ref, (dq_acc[...] * SCALE).astype(BF16))


def attend_short(lengths_ref, q_ref, k_ref, v_ref, g_ref, o_ref, dq_ref, dk_ref, dv_ref):
    heads = HQ // HK
    lanes = heads * SHORT_DEV
    key = lax.broadcasted_iota(jnp.int32, (SHORT_DEV, lanes), 0)
    row = jnp.concatenate(
        [lax.broadcasted_iota(jnp.int32, (SHORT_DEV, SHORT_DEV), 1)] * heads, 1)
    end = 0
    key_segment = jnp.zeros_like(key)
    row_segment = jnp.zeros_like(row)
    for j in range(4):
        end = end + lengths_ref[0, j]
        key_segment = key_segment + (key >= end).astype(jnp.int32)
        row_segment = row_segment + (row >= end).astype(jnp.int32)
    masked = jnp.where((key > row) | (key_segment != row_segment), MASKED, 0.0)

    def one(c, carry):
        mine = pl.ds(pl.multiple_of(c * DH, DH), DH)

        def col(h):
            return pl.ds(pl.multiple_of((c * heads + h) * DH, DH), DH)

        def gather(ref):
            return jnp.concatenate([ref[:SHORT_DEV, col(h)] for h in range(heads)], 0)

        q = gather(q_ref)
        g = gather(g_ref)
        k = k_ref[:SHORT_DEV, mine]
        v = v_ref[:SHORT_DEV, mine]
        s = dot(k, q, 1, 1) + masked
        p = jnp.exp2((s - jnp.max(s, axis=0, keepdims=True)) * SCALE2)
        weights = p * (1.0 / jnp.sum(p, axis=0, keepdims=True))
        w = weights.astype(BF16)
        out = dot(v.T, w, 1, 0).astype(BF16)
        dv_ref[:, mine] = dot(w, g, 1, 0).astype(BF16)
        product = jnp.sum(g.T.astype(F32) * out.astype(F32), axis=0, keepdims=True)
        ds = (weights * (dot(v, g, 1, 1) - product)).astype(BF16)
        dq = (dot(k.T, ds, 1, 0) * SCALE).astype(BF16)
        dk_ref[:, mine] = (dot(ds, q, 1, 0) * SCALE).astype(BF16)
        out = out.T
        dq = dq.T
        for h in range(heads):
            o_ref[:, col(h)] = out[h * SHORT_DEV:(h + 1) * SHORT_DEV]
            dq_ref[:, col(h)] = dq[h * SHORT_DEV:(h + 1) * SHORT_DEV]
        return carry

    lax.fori_loop(0, HK, one, 0)


def kernel(lengths_ref, doc_len_ref, doc_group_ref, doc_off_ref, q_hbm, k_hbm, v_hbm, g_hbm,
           back_a, back_b, so_ref, sdq_ref, sdk_ref, sdv_ref,
           q_ref, k_ref, v_ref, g_ref, send_a, send_b, got_a, got_b, qd, gd, kd, vd, kt, vt, od, dqd,
           dk_acc, dv_acc, s_buf, o_acc, dq_acc, edge,
           send_sem, recv_sem, own_sem, load_sem):
    dp = lax.axis_index("dp")
    ctx = lax.axis_index("ctx")
    me = dp * 4 + ctx
    my_place = position_of(dp, ctx)
    barrier = pltpu.get_barrier_semaphore()

    def greet(*to):
        pl.semaphore_signal(barrier, inc=1, device_id=to, device_id_type=MESH)

    each_partner(dp, ctx, greet)
    loads = [
        pltpu.make_async_copy(src, dst, load_sem.at[n])
        for n, (src, dst) in enumerate(
            ((q_hbm, q_ref), (g_hbm, g_ref), (k_hbm, k_ref), (v_hbm, v_ref)))]
    for load in loads:
        load.start()

    def pack(out, first, with_keys):
        def body(b, carry):
            base = pl.multiple_of(SHORT_DEV + SLAB * b, 16)
            for c in range(HK):
                col = (c * (HQ // HK) + first) * DH
                parts = [(q_ref, col), (q_ref, col + DH), (g_ref, col), (g_ref, col + DH)]
                if with_keys:
                    parts += [(k_ref, c * DH), (v_ref, c * DH)]
                for n, (ref, at) in enumerate(parts):
                    x = ref[pl.ds(base, SLAB), at:at + DH]
                    for j in range(8):
                        out[(b * 8 + j) * 4 + c, PIECE * n:PIECE * (n + 1), :] = (
                            x[PIECE * j:PIECE * (j + 1)])
            return carry

        lax.fori_loop(0, GROUPS // 8, body, 0)

    def exchange(slot, src, dst, src_index, dst_index):
        def send(*to):
            pltpu.make_async_remote_copy(
                src_ref=src.at[src_index(*to)], dst_ref=dst.at[dst_index],
                send_sem=send_sem.at[slot], recv_sem=recv_sem.at[slot],
                device_id=to, device_id_type=MESH).start()

        each_partner(dp, ctx, send)
        pltpu.make_async_copy(
            src.at[src_index(dp, ctx)], dst.at[dst_index], own_sem.at[slot]).start()

    def wait_bytes(ref, sem):
        whole = ref.at[pl.ds(0, N_DEV - 1)]
        pltpu.make_async_copy(whole, whole, sem).wait()

    def received(slot, src, dst):
        pltpu.make_async_copy(src.at[0], dst.at[0], own_sem.at[slot]).wait()
        wait_bytes(dst, recv_sem.at[slot])

    send_a[:, 96:, :] = jnp.zeros((N_DEV, ROWS_A - 96, DH), BF16)
    for load in loads:
        load.wait()
    pack(send_a, 0, True)
    pl.semaphore_wait(barrier, N_DEV - 1)
    exchange(0, send_a, got_a, lambda d, c: d * 4 + c, my_place)
    pack(send_b, PAIR, False)
    attend_short(lengths_ref, q_ref, k_ref, v_ref, g_ref, so_ref, sdq_ref, sdk_ref, sdv_ref)

    def find(i, acc):
        mine = (doc_group_ref[i] == dp) & (doc_len_ref[i] > 0)
        return acc + jnp.where(mine, doc_off_ref[i], 0)

    bound = lax.fori_loop(0, doc_len_ref.shape[0], find, jnp.int32(0))
    dk_acc[...] = jnp.zeros_like(dk_acc)
    dv_acc[...] = jnp.zeros_like(dv_acc)

    def spread(src, dests):
        def body(b, carry):
            at = pl.ds(pl.multiple_of(b * SLAB, 16), SLAB)
            for n, (ref, h) in enumerate(dests):
                for j in range(8):
                    edge[n, PIECE * j:PIECE * (j + 1), :] = (
                        src[b * 8 + j, PIECE * n:PIECE * (n + 1), :])
                if h is None:
                    ref[at, :] = edge[n]
                else:
                    ref[h, at, :] = edge[n]
            return carry

        lax.fori_loop(0, N_DEV // 8, body, 0)

    def collect(out, load):
        def body(b, carry):
            at = pl.ds(pl.multiple_of(b * SLAB, 16), SLAB)
            for n, x in enumerate(load(at)):
                for j in range(8):
                    out[b * 8 + j, PIECE * n:PIECE * (n + 1), :] = x[PIECE * j:PIECE * (j + 1)]
            return carry

        lax.fori_loop(0, N_DEV // 8, body, 0)

    def attend():
        def body(i, carry):
            attend_tile(i, bound, qd, gd, kd, vd, kt, vt, od, dqd,
                        dk_acc, dv_acc, s_buf, o_acc, dq_acc)
            return carry

        lax.fori_loop(0, SPAN // TILE, body, 0)

    query_side = [(qd, 0), (qd, 1), (gd, 0), (gd, 1)]
    received(0, send_a, got_a)
    exchange(1, send_b, got_b, lambda d, c: d * 4 + c, my_place)
    spread(got_a, query_side + [(kd, None), (vd, None)])
    kt[...] = kd[...].T
    vt[...] = vd[...].T
    attend()

    received(1, send_b, got_b)
    wait_bytes(send_b, send_sem.at[1])
    collect(send_b, lambda at: [od[0, at, :], od[1, at, :], dqd[0, at, :], dqd[1, at, :]])
    exchange(2, send_b, back_a, position_of, me)

    spread(got_b, query_side)
    attend()
    wait_bytes(send_a, send_sem.at[0])
    collect(send_a, lambda at: [
        od[0, at, :], od[1, at, :], dqd[0, at, :], dqd[1, at, :],
        (dk_acc[at, :] * SCALE).astype(BF16), dv_acc[at, :].astype(BF16)])
    exchange(3, send_a, back_b, position_of, me)

    received(2, send_b, back_a)
    wait_bytes(send_b, send_sem.at[2])
    received(3, send_a, back_b)
    wait_bytes(send_a, send_sem.at[3])


def place(back_a, back_b, so_ref, sdq_ref, sdk_ref, sdv_ref, o_ref, dq_ref, dk_ref, dv_ref, edge):
    o_ref[:SHORT_DEV, :] = so_ref[...]
    dq_ref[:SHORT_DEV, :] = sdq_ref[...]
    dk_ref[:SHORT_DEV, :] = sdk_ref[...]
    dv_ref[:SHORT_DEV, :] = sdv_ref[...]
    moves = []
    for half, src in enumerate((back_a, back_b)):
        for n, ref in enumerate((o_ref, o_ref, dq_ref, dq_ref)):
            moves.append((src, n, ref, (half * 2 + n % 2) * DH))
    moves += [(back_b, 4, dk_ref, 0), (back_b, 5, dv_ref, 0)]

    def body(b, carry):
        at = pl.ds(pl.multiple_of(SHORT_DEV + b * SLAB, 16), SLAB)
        for m, (src, n, ref, col) in enumerate(moves):
            for j in range(8):
                edge[m, PIECE * j:PIECE * (j + 1), :] = (
                    src[b * 8 + j, 0, PIECE * n:PIECE * (n + 1), :])
            ref[at, col:col + DH] = edge[m]
        return carry

    lax.fori_loop(0, GROUPS // 8, body, 0)


def per_device(queries, keys, values, out_grad, short_lengths, doc_lengths, doc_group, doc_offset):
    vmem = pl.BlockSpec(memory_space=pltpu.VMEM)
    smem = pl.BlockSpec(memory_space=pltpu.SMEM)
    hbm = pl.BlockSpec(memory_space=pl.ANY)

    def shape(*dims):
        return jax.ShapeDtypeStruct(dims, BF16)

    results = pl.pallas_call(
        kernel,
        out_shape=[
            shape(N_DEV, ROWS_B, DH), shape(N_DEV, ROWS_A, DH),
            shape(SHORT_DEV, HQ * DH), shape(SHORT_DEV, HQ * DH),
            shape(SHORT_DEV, HK * DH), shape(SHORT_DEV, HK * DH)],
        in_specs=[smem] * 4 + [hbm] * 4,
        out_specs=[hbm, hbm] + [vmem] * 4,
        scratch_shapes=[
            pltpu.VMEM((ROWS, HQ * DH), BF16), pltpu.VMEM((ROWS, HK * DH), BF16),
            pltpu.VMEM((ROWS, HK * DH), BF16), pltpu.VMEM((ROWS, HQ * DH), BF16),
            pltpu.VMEM((N_DEV, ROWS_A, DH), BF16), pltpu.VMEM((N_DEV, ROWS_B, DH), BF16),
            pltpu.VMEM((N_DEV, ROWS_A, DH), BF16), pltpu.VMEM((N_DEV, ROWS_B, DH), BF16),
            pltpu.VMEM((PAIR, SPAN, DH), BF16), pltpu.VMEM((PAIR, SPAN, DH), BF16),
            pltpu.VMEM((SPAN, DH), BF16), pltpu.VMEM((SPAN, DH), BF16),
            pltpu.VMEM((DH, SPAN), BF16), pltpu.VMEM((DH, SPAN), BF16),
            pltpu.VMEM((PAIR, SPAN, DH), BF16), pltpu.VMEM((PAIR, SPAN, DH), BF16),
            pltpu.VMEM((SPAN, DH), F32), pltpu.VMEM((SPAN, DH), F32),
            pltpu.VMEM((SPAN, PAIR * TILE), F32),
            pltpu.VMEM((DH, PAIR * TILE), F32), pltpu.VMEM((DH, PAIR * TILE), F32),
            pltpu.VMEM((6, SLAB, DH), BF16),
            pltpu.SemaphoreType.DMA((4,)), pltpu.SemaphoreType.DMA((4,)),
            pltpu.SemaphoreType.DMA((4,)), pltpu.SemaphoreType.DMA((4,))],
        compiler_params=pltpu.CompilerParams(
            collective_id=0, has_side_effects=True, vmem_limit_bytes=60 << 20),
        name="relay_and_attend",
    )(short_lengths, doc_lengths, doc_group, doc_offset, queries, keys, values, out_grad)

    back_a, back_b, *short = results
    heads = HQ // HK

    def back_spec(rows):
        return pl.BlockSpec((GROUPS, 1, rows, DH), lambda c: (0, c, 0, 0))

    def col_spec(rows, width):
        return pl.BlockSpec((rows, width), lambda c: (0, c))

    return tuple(pl.pallas_call(
        place,
        grid=(HK,),
        out_shape=[shape(ROWS, HQ * DH), shape(ROWS, HQ * DH),
                   shape(ROWS, HK * DH), shape(ROWS, HK * DH)],
        in_specs=[back_spec(ROWS_B), back_spec(ROWS_A),
                  col_spec(SHORT_DEV, heads * DH), col_spec(SHORT_DEV, heads * DH),
                  col_spec(SHORT_DEV, DH), col_spec(SHORT_DEV, DH)],
        out_specs=[col_spec(ROWS, heads * DH), col_spec(ROWS, heads * DH),
                   col_spec(ROWS, DH), col_spec(ROWS, DH)],
        scratch_shapes=[pltpu.VMEM((10, SLAB, DH), BF16)],
        compiler_params=pltpu.CompilerParams(vmem_limit_bytes=60 << 20),
        name="place_outputs",
    )(back_a.reshape(GROUPS, N_DEV // GROUPS, ROWS_B, DH),
      back_b.reshape(GROUPS, N_DEV // GROUPS, ROWS_A, DH), *short))


def solution(mesh):
    rows = P(("dp", "ctx"), None)
    return jax.shard_map(
        per_device, mesh=mesh,
        in_specs=(rows, rows, rows, rows, rows, P(), P(), P()),
        out_specs=(rows, rows, rows, rows), check_vma=False)
```

time: 765 us -> 171 us (0.22); the launches traced: 754 us -> 171 us
  matrix products: 249 us -> 0 us
  local copies, waits for them, and re-layouts: 227 us -> 0 us
  Pallas kernels: 0 us -> 170 us
  other arithmetic: 93.8 us -> 0 us
  waiting for transfers between devices: 87.6 us -> 0 us
  starting transfers between devices: 43.8 us -> 0 us
  blocking collectives: 23.6 us -> 0 us
  loops' own time: 14.9 us -> 0 us
  between operations: 14.4 us -> 0.74 us
    dot_general x56 -> x0, matrix products: 249 us -> none  [the longest x16 75.2 us: tile_scores(): jnp.einsum('tqgd,tkd->tgqk', tile_query, tile_key, preferred_element_type...]
    pallas_call x0 -> x2, Pallas kernels: none -> 170 us  [the longest x1 163 us: per_device(): pl.pallas_call(kernel, out_shape=[shape(N_DEV, ROWS_B, DH), shape(N_DEV,...]
    all_to_all x7 -> x0, waiting for transfers between devices: 87.5 us -> none  [the longest x1 29.2 us: per_device(): lax.all_to_all(pieces(queries[SHORT_DEV:]), 'dp', split_axis=0, concat_ax...]
    reduce_sum x28 -> x0, other arithmetic: 64.8 us -> none  [the longest x8 39.6 us: forward_one_head(): block_sum = collect(pick, jnp.sum(shifted, axis=3))]
    gather x54 -> x0, local copies, waits for them, and re-layouts: 64.7 us -> none  [the longest x2 12.4 us: per_device(): block_seg = segments[block_pos]]
    all_to_all x7 -> x0, starting transfers between devices: 43.6 us -> none  [the longest x1 7.54 us: per_device(): lax.all_to_all(for_sending(pieces(long_dv)), 'dp', split_axis=0, concat_a...]
    squeeze x24 -> x0, local copies, waits for them, and re-layouts: 32.3 us -> none  [the longest x20 29.5 us: forward_tiles(): lax.map(forward_one_head, (head_split(query_blocks), key_split(key_blocks...]
    another operation x9 -> x0, local copies, waits for them, and re-layouts: 29.3 us -> none  [the longest x4 13.3 us: head_split(): blocks.reshape(count, rows, HK, HQ // HK, DH).transpose(2, 0, 1, 3, 4)]
  transfers between devices with their start and end apart: 11 -> 0, of which waited for: 6 -> 0; matrix products, arithmetic and copies ran while one was open for 21% -> 0% of each run, Pallas kernels for 0% -> 0%
where the time goes in v1:
time: 171 us
  Pallas kernels  170 us (99%)
    pallas_call x1, Pallas kernels, per_device(): pl.pallas_call(kernel, out_shape=[shape(N_DEV, ROWS_B, DH), shape(N_DEV,...  163 us
    pallas_call x1, Pallas kernels, per_device(): pl.pallas_call(place, grid=(HK,), out_shape=[shape(ROWS, HQ * DH), shape(...  7.63 us

profile of v1, /device:TPU:1, one launch (start us, length us, event | category | flops | bytes accessed | tf_op | source)
XLA Modules:
  0.0 170.9 jit_solution(15022110532278342968)
XLA Ops:
  0.6 162.5 %relay_and_attend.1 = (bf16[128,72,128]{2,1,0:T(8,128)(2,1)}, bf16[128,112,128]{2,1,0:T(8,128)(2,1)}, bf16[128,2048]{1,0:T(8,128)(2,1)}, bf16[128,2048]{1,0:T(8,...) custom-call(s32[1,4]{1,0:T(1,128)} %lengths_ref.1, s32[64]{0:T(128)} %doc_len_ref.1, s32[64]{0:T(128)} %doc_group_ref.1, ...), custom_call_target="tpu_custom_call" | custom-call | tf_op jit(solution)/shard_map/relay_and_attend/pallas_call | solution.py:392
  163.2 7.6 %place_outputs.1 = (bf16[704,2048]{1,0:T(8,128)(2,1)}, bf16[704,2048]{1,0:T(8,128)(2,1)}, bf16[704,512]{1,0:T(8,128)(2,1)}, bf16[704,512]{1,0:T(8,128)(2,1)}) custom-call(bf16[32,4,72,128]{3,2,1,0:T(8,128)(2,1)} %bitcast.3, bf16[32,4,112,128]{3,2,1,0:T(8,128)(2,1)} %bitcast.2, bf16[128,2048]{1,0:T(8,128)(2,1)} %get-tuple-element.12.so_ref, ...), custom_call_target="tpu_custom_call" | custom-call | tf_op jit(solution)/shard_map/place_outputs/pallas_call | solution.py:429

commit v2 on v1

--- a/solution.py
+++ b/solution.py
@@ -53,18 +53,20 @@
     return jnp.where(dp < 16, ctx * 16 + dp, (7 - ctx) * 16 + dp - 16)
 
 
+EARLY = 7
+
 TURNS = ((1, 0), (0, 1), (3, 0), (0, 3), (1, 3), (3, 1), (2, 2), (0, 2),
          (2, 0), (1, 1), (3, 3), (1, 2), (3, 2), (2, 1), (2, 3), (0, 0))
 
 
-def each_partner(dp, ctx, body):
+def each_partner(dp, ctx, body, late=None):
     def wrap(value, size):
         return jnp.where(value >= size, value - size, value)
 
     xs = [wrap(ctx + i, 4) for i in range(4)]
     ys = [wrap(lax.rem(dp // 2, 4) + i, 4) * 2 for i in range(4)]
 
-    def turn(j, turns):
+    def turn(j, turns, body):
         z = wrap(dp // 8 + lax.rem(j, 4), 4)
         core = wrap(lax.rem(dp, 2) + j // 4, 2)
         zs = [wrap(z + i, 4) * 8 for i in range(4)]
@@ -72,12 +74,16 @@
         for x, y in turns:
             body(zs[(x + y) % 4] + ys[y] + cores[x % 2], xs[x])
 
-    def step(j, carry):
-        turn(j, TURNS)
-        return carry
-
-    turn(0, TURNS[:-1])
-    lax.fori_loop(1, 8, step, 0)
+    def step(call):
+        def one(j, carry):
+            turn(j, TURNS, call)
+            return carry
+
+        return one
+
+    turn(0, TURNS[:-1], body)
+    lax.fori_loop(1, EARLY, step(body), 0)
+    lax.fori_loop(EARLY, 8, step(late or body), 0)
 
 
 def attend_tile(i, bound, q_ref, g_ref, k_ref, v_ref, kt_ref, vt_ref, o_ref, dq_ref,
@@ -224,8 +230,8 @@
 
 
 def kernel(lengths_ref, doc_len_ref, doc_group_ref, doc_off_ref, q_hbm, k_hbm, v_hbm, g_hbm,
-           back_a, back_b, so_ref, sdq_ref, sdk_ref, sdv_ref,
-           q_ref, k_ref, v_ref, g_ref, send_a, send_b, got_a, got_b, qd, gd, kd, vd, kt, vt, od, dqd,
+           back_a, back_b, so_hbm, sdq_hbm, sdk_hbm, sdv_hbm,
+           q_ref, k_ref, v_ref, g_ref, so_ref, sdq_ref, sdk_ref, sdv_ref, send_a, send_b, got_a, got_b, qd, gd, kd, vd, kt, vt, od, dqd,
            dk_acc, dv_acc, s_buf, o_acc, dq_acc, edge,
            send_sem, recv_sem, own_sem, load_sem):
     dp = lax.axis_index("dp")
@@ -263,23 +269,35 @@
         lax.fori_loop(0, GROUPS // 8, body, 0)
 
     def exchange(slot, src, dst, src_index, dst_index):
-        def send(*to):
-            pltpu.make_async_remote_copy(
-                src_ref=src.at[src_index(*to)], dst_ref=dst.at[dst_index],
-                send_sem=send_sem.at[slot], recv_sem=recv_sem.at[slot],
-                device_id=to, device_id_type=MESH).start()
-
-        each_partner(dp, ctx, send)
+        def send_on(recv):
+            def send(*to):
+                pltpu.make_async_remote_copy(
+                    src_ref=src.at[src_index(*to)], dst_ref=dst.at[dst_index],
+                    send_sem=send_sem.at[slot], recv_sem=recv_sem.at[recv],
+                    device_id=to, device_id_type=MESH).start()
+
+            return send
+
+        each_partner(dp, ctx, send_on(slot), send_on(slot + 4) if slot < 2 else None)
         pltpu.make_async_copy(
             src.at[src_index(dp, ctx)], dst.at[dst_index], own_sem.at[slot]).start()
 
-    def wait_bytes(ref, sem):
-        whole = ref.at[pl.ds(0, N_DEV - 1)]
+    def wait_bytes(ref, sem, count=N_DEV - 1):
+        whole = ref.at[pl.ds(0, count)]
         pltpu.make_async_copy(whole, whole, sem).wait()
 
+    def own_copy(slot, src, dst):
+        return pltpu.make_async_copy(src.at[0], dst.at[0], own_sem.at[slot])
+
+    def mostly_received(slot, dst):
+        wait_bytes(dst, recv_sem.at[slot], 16 * EARLY - 1)
+
     def received(slot, src, dst):
-        pltpu.make_async_copy(src.at[0], dst.at[0], own_sem.at[slot]).wait()
-        wait_bytes(dst, recv_sem.at[slot])
+        own_copy(slot, src, dst).wait()
+        if slot < 2:
+            wait_bytes(dst, recv_sem.at[slot + 4], 16 * (8 - EARLY))
+        else:
+            wait_bytes(dst, recv_sem.at[slot])
 
     send_a[:, 96:, :] = jnp.zeros((N_DEV, ROWS_A - 96, DH), BF16)
     for load in loads:
@@ -289,6 +307,12 @@
     exchange(0, send_a, got_a, lambda d, c: d * 4 + c, my_place)
     pack(send_b, PAIR, False)
     attend_short(lengths_ref, q_ref, k_ref, v_ref, g_ref, so_ref, sdq_ref, sdk_ref, sdv_ref)
+    stores = [
+        pltpu.make_async_copy(src, dst, load_sem.at[4 + n])
+        for n, (src, dst) in enumerate(
+            ((so_ref, so_hbm), (sdq_ref, sdq_hbm), (sdk_ref, sdk_hbm), (sdv_ref, sdv_hbm)))]
+    for store in stores:
+        store.start()
 
     def find(i, acc):
         mine = (doc_group_ref[i] == dp) & (doc_len_ref[i] > 0)
@@ -332,18 +356,20 @@
         lax.fori_loop(0, SPAN // TILE, body, 0)
 
     query_side = [(qd, 0), (qd, 1), (gd, 0), (gd, 1)]
+    mostly_received(0, got_a)
+    exchange(1, send_b, got_b, lambda d, c: d * 4 + c, my_place)
     received(0, send_a, got_a)
-    exchange(1, send_b, got_b, lambda d, c: d * 4 + c, my_place)
     spread(got_a, query_side + [(kd, None), (vd, None)])
     kt[...] = kd[...].T
     vt[...] = vd[...].T
     attend()
 
-    received(1, send_b, got_b)
     wait_bytes(send_b, send_sem.at[1])
+    own_copy(1, send_b, got_b).wait()
     collect(send_b, lambda at: [od[0, at, :], od[1, at, :], dqd[0, at, :], dqd[1, at, :]])
+    mostly_received(1, got_b)
     exchange(2, send_b, back_a, position_of, me)
-
+    wait_bytes(got_b, recv_sem.at[5], 16 * (8 - EARLY))
     spread(got_b, query_side)
     attend()
     wait_bytes(send_a, send_sem.at[0])
@@ -352,13 +378,15 @@
         (dk_acc[at, :] * SCALE).astype(BF16), dv_acc[at, :].astype(BF16)])
     exchange(3, send_a, back_b, position_of, me)
 
+    for store in stores:
+        store.wait()
     received(2, send_b, back_a)
     wait_bytes(send_b, send_sem.at[2])
     received(3, send_a, back_b)
     wait_bytes(send_a, send_sem.at[3])
 
 
-def place(back_a, back_b, so_ref, sdq_ref, sdk_ref, sdv_ref, o_ref, dq_ref, dk_ref, dv_ref, edge):
+def place(back_a, back_b, so_ref, sdq_ref, sdk_ref, sdv_ref, o_ref, dq_ref, dk_ref, dv_ref):
     o_ref[:SHORT_DEV, :] = so_ref[...]
     dq_ref[:SHORT_DEV, :] = sdq_ref[...]
     dk_ref[:SHORT_DEV, :] = sdk_ref[...]
@@ -369,20 +397,13 @@
             moves.append((src, n, ref, (half * 2 + n % 2) * DH))
     moves += [(back_b, 4, dk_ref, 0), (back_b, 5, dv_ref, 0)]
 
-    def body(b, carry):
-        at = pl.ds(pl.multiple_of(SHORT_DEV + b * SLAB, 16), SLAB)
-        for m, (src, n, ref, col) in enumerate(moves):
-            for j in range(8):
-                edge[m, PIECE * j:PIECE * (j + 1), :] = (
-                    src[b * 8 + j, 0, PIECE * n:PIECE * (n + 1), :])
-            ref[at, col:col + DH] = edge[m]
-        return carry
-
-    lax.fori_loop(0, GROUPS // 8, body, 0)
+    for g in range(GROUPS):
+        at = SHORT_DEV + PIECE * g
+        for src, n, ref, col in moves:
+            ref[at:at + PIECE, col:col + DH] = src[g, 0, PIECE * n:PIECE * (n + 1), :]
 
 
 def per_device(queries, keys, values, out_grad, short_lengths, doc_lengths, doc_group, doc_offset):
-    vmem = pl.BlockSpec(memory_space=pltpu.VMEM)
     smem = pl.BlockSpec(memory_space=pltpu.SMEM)
     hbm = pl.BlockSpec(memory_space=pl.ANY)
 
@@ -396,10 +417,12 @@
             shape(SHORT_DEV, HQ * DH), shape(SHORT_DEV, HQ * DH),
             shape(SHORT_DEV, HK * DH), shape(SHORT_DEV, HK * DH)],
         in_specs=[smem] * 4 + [hbm] * 4,
-        out_specs=[hbm, hbm] + [vmem] * 4,
+        out_specs=[hbm] * 6,
         scratch_shapes=[
             pltpu.VMEM((ROWS, HQ * DH), BF16), pltpu.VMEM((ROWS, HK * DH), BF16),
             pltpu.VMEM((ROWS, HK * DH), BF16), pltpu.VMEM((ROWS, HQ * DH), BF16),
+            pltpu.VMEM((SHORT_DEV, HQ * DH), BF16), pltpu.VMEM((SHORT_DEV, HQ * DH), BF16),
+            pltpu.VMEM((SHORT_DEV, HK * DH), BF16), pltpu.VMEM((SHORT_DEV, HK * DH), BF16),
             pltpu.VMEM((N_DEV, ROWS_A, DH), BF16), pltpu.VMEM((N_DEV, ROWS_B, DH), BF16),
             pltpu.VMEM((N_DEV, ROWS_A, DH), BF16), pltpu.VMEM((N_DEV, ROWS_B, DH), BF16),
             pltpu.VMEM((PAIR, SPAN, DH), BF16), pltpu.VMEM((PAIR, SPAN, DH), BF16),
@@ -410,8 +433,8 @@
             pltpu.VMEM((SPAN, PAIR * TILE), F32),
             pltpu.VMEM((DH, PAIR * TILE), F32), pltpu.VMEM((DH, PAIR * TILE), F32),
             pltpu.VMEM((6, SLAB, DH), BF16),
-            pltpu.SemaphoreType.DMA((4,)), pltpu.SemaphoreType.DMA((4,)),
-            pltpu.SemaphoreType.DMA((4,)), pltpu.SemaphoreType.DMA((4,))],
+            pltpu.SemaphoreType.DMA((4,)), pltpu.SemaphoreType.DMA((6,)),
+            pltpu.SemaphoreType.DMA((4,)), pltpu.SemaphoreType.DMA((8,))],
         compiler_params=pltpu.CompilerParams(
             collective_id=0, has_side_effects=True, vmem_limit_bytes=60 << 20),
         name="relay_and_attend",
@@ -436,7 +459,6 @@
                   col_spec(SHORT_DEV, DH), col_spec(SHORT_DEV, DH)],
         out_specs=[col_spec(ROWS, heads * DH), col_spec(ROWS, heads * DH),
                    col_spec(ROWS, DH), col_spec(ROWS, DH)],
-        scratch_shapes=[pltpu.VMEM((10, SLAB, DH), BF16)],
         compiler_params=pltpu.CompilerParams(vmem_limit_bytes=60 << 20),
         name="place_outputs",
     )(back_a.reshape(GROUPS, N_DEV // GROUPS, ROWS_B, DH),

time: 171 us -> 168 us (0.982)
  Pallas kernels: 170 us -> 165 us
    pallas_call x1, Pallas kernels: 163 us -> 159 us  [per_device(): pl.pallas_call(kernel, out_shape=[shape(N_DEV, ROWS_B, DH), shape(N_DEV,...]
where the time goes in v2:
time: 168 us; the launch traced here: 166 us
  Pallas kernels  165 us (98%)
    pallas_call x1, Pallas kernels, per_device(): pl.pallas_call(kernel, out_shape=[shape(N_DEV, ROWS_B, DH), shape(N_DEV,...  159 us
    pallas_call x1, Pallas kernels, per_device(): pl.pallas_call(place, grid=(HK,), out_shape=[shape(ROWS, HQ * DH), shape(...  6.91 us

profile of v2, /device:TPU:1, one launch (start us, length us, event | category | flops | bytes accessed | tf_op | source)
XLA Modules:
  0.0 166.2 jit_solution(11555718510940660970)
XLA Ops:
  0.6 158.5 %relay_and_attend.1 = (bf16[128,72,128]{2,1,0:T(8,128)(2,1)}, bf16[128,112,128]{2,1,0:T(8,128)(2,1)}, bf16[128,2048]{1,0:T(8,128)(2,1)}, bf16[128,2048]{1,0:T(8,...) custom-call(s32[1,4]{1,0:T(1,128)} %lengths_ref.1, s32[64]{0:T(128)} %doc_len_ref.1, s32[64]{0:T(128)} %doc_group_ref.1, ...), custom_call_target="tpu_custom_call" | custom-call | tf_op jit(solution)/shard_map/relay_and_attend/pallas_call | solution.py:413
  159.2 6.9 %place_outputs.1 = (bf16[704,2048]{1,0:T(8,128)(2,1)}, bf16[704,2048]{1,0:T(8,128)(2,1)}, bf16[704,512]{1,0:T(8,128)(2,1)}, bf16[704,512]{1,0:T(8,128)(2,1)}) custom-call(bf16[32,4,72,128]{3,2,1,0:T(8,128)(2,1)} %bitcast.3, bf16[32,4,112,128]{3,2,1,0:T(8,128)(2,1)} %bitcast.2, bf16[128,2048]{1,0:T(8,128)(2,1)} %get-tuple-element.12.so_ref, ...), custom_call_target="tpu_custom_call" | custom-call | tf_op jit(solution)/shard_map/place_outputs/pallas_call | solution.py:452

commit v3 on v2

--- a/solution.py
+++ b/solution.py
@@ -386,21 +386,59 @@
     wait_bytes(send_a, send_sem.at[3])
 
 
-def place(back_a, back_b, so_ref, sdq_ref, sdk_ref, sdv_ref, o_ref, dq_ref, dk_ref, dv_ref):
-    o_ref[:SHORT_DEV, :] = so_ref[...]
-    dq_ref[:SHORT_DEV, :] = sdq_ref[...]
-    dk_ref[:SHORT_DEV, :] = sdk_ref[...]
-    dv_ref[:SHORT_DEV, :] = sdv_ref[...]
+def place(back_a, back_b, so_ref, sdq_ref, sdk_ref, sdv_ref, o_ref, dq_ref, dk_ref, dv_ref,
+          a_buf, b_buf, o_buf, dq_buf, dk_buf, dv_buf, so_buf, sdq_buf, sdk_buf, sdv_buf,
+          in_sem, out_sem, short_sem):
+    heads = HQ // HK
+    steps = GROUPS // 8
+    slots = N_DEV // steps
+    shorts = ((so_ref, so_buf, o_ref), (sdq_ref, sdq_buf, dq_ref),
+              (sdk_ref, sdk_buf, dk_ref), (sdv_ref, sdv_buf, dv_ref))
+    fetched = [
+        pltpu.make_async_copy(src, buf, short_sem.at[0, n])
+        for n, (src, buf, _) in enumerate(shorts)]
+    loads = []
+    for b in range(steps):
+        part = pl.ds(b * slots, slots)
+        loads.append([
+            pltpu.make_async_copy(back_a.at[part], a_buf.at[part], in_sem.at[b, 0]),
+            pltpu.make_async_copy(back_b.at[part], b_buf.at[part], in_sem.at[b, 1])])
+        for load in loads[b] + (fetched if b == 0 else []):
+            load.start()
     moves = []
-    for half, src in enumerate((back_a, back_b)):
-        for n, ref in enumerate((o_ref, o_ref, dq_ref, dq_ref)):
-            moves.append((src, n, ref, (half * 2 + n % 2) * DH))
-    moves += [(back_b, 4, dk_ref, 0), (back_b, 5, dv_ref, 0)]
-
-    for g in range(GROUPS):
-        at = SHORT_DEV + PIECE * g
-        for src, n, ref, col in moves:
-            ref[at:at + PIECE, col:col + DH] = src[g, 0, PIECE * n:PIECE * (n + 1), :]
+    for half, src in enumerate((a_buf, b_buf)):
+        for n, buf in enumerate((o_buf, o_buf, dq_buf, dq_buf)):
+            moves.append((src, n, buf, heads, half * 2 + n % 2))
+    moves += [(b_buf, 4, dk_buf, 1, 0), (b_buf, 5, dv_buf, 1, 0)]
+
+    copies = []
+    for b in range(steps):
+        for load in loads[b]:
+            load.wait()
+
+        def columns(c, carry):
+            for j in range(8):
+                for src, n, buf, width, at in moves:
+                    col = pl.multiple_of((c * width + at) * DH, DH)
+                    buf[b, PIECE * j:PIECE * (j + 1), pl.ds(col, DH)] = (
+                        src[(b * 8 + j) * HK + c, PIECE * n:PIECE * (n + 1), :])
+            return carry
+
+        lax.fori_loop(0, HK, columns, 0)
+        rows = pl.ds(SHORT_DEV + b * SLAB, SLAB)
+        for n, (buf, dst) in enumerate(
+                ((o_buf, o_ref), (dq_buf, dq_ref), (dk_buf, dk_ref), (dv_buf, dv_ref))):
+            copy = pltpu.make_async_copy(buf.at[b], dst.at[rows], out_sem.at[b, n])
+            copy.start()
+            copies.append(copy)
+        if b == 0:
+            for n, (_, buf, dst) in enumerate(shorts):
+                fetched[n].wait()
+                copy = pltpu.make_async_copy(buf, dst.at[pl.ds(0, SHORT_DEV)], short_sem.at[1, n])
+                copy.start()
+                copies.append(copy)
+    for copy in copies:
+        copy.wait()
 
 
 def per_device(queries, keys, values, out_grad, short_lengths, doc_lengths, doc_group, doc_offset):
@@ -440,29 +478,24 @@
         name="relay_and_attend",
     )(short_lengths, doc_lengths, doc_group, doc_offset, queries, keys, values, out_grad)
 
-    back_a, back_b, *short = results
-    heads = HQ // HK
-
-    def back_spec(rows):
-        return pl.BlockSpec((GROUPS, 1, rows, DH), lambda c: (0, c, 0, 0))
-
-    def col_spec(rows, width):
-        return pl.BlockSpec((rows, width), lambda c: (0, c))
-
+    steps = GROUPS // 8
     return tuple(pl.pallas_call(
         place,
-        grid=(HK,),
         out_shape=[shape(ROWS, HQ * DH), shape(ROWS, HQ * DH),
                    shape(ROWS, HK * DH), shape(ROWS, HK * DH)],
-        in_specs=[back_spec(ROWS_B), back_spec(ROWS_A),
-                  col_spec(SHORT_DEV, heads * DH), col_spec(SHORT_DEV, heads * DH),
-                  col_spec(SHORT_DEV, DH), col_spec(SHORT_DEV, DH)],
-        out_specs=[col_spec(ROWS, heads * DH), col_spec(ROWS, heads * DH),
-                   col_spec(ROWS, DH), col_spec(ROWS, DH)],
+        in_specs=[hbm] * 6,
+        out_specs=[hbm] * 4,
+        scratch_shapes=[
+            pltpu.VMEM((N_DEV, ROWS_B, DH), BF16), pltpu.VMEM((N_DEV, ROWS_A, DH), BF16),
+            pltpu.VMEM((steps, SLAB, HQ * DH), BF16), pltpu.VMEM((steps, SLAB, HQ * DH), BF16),
+            pltpu.VMEM((steps, SLAB, HK * DH), BF16), pltpu.VMEM((steps, SLAB, HK * DH), BF16),
+            pltpu.VMEM((SHORT_DEV, HQ * DH), BF16), pltpu.VMEM((SHORT_DEV, HQ * DH), BF16),
+            pltpu.VMEM((SHORT_DEV, HK * DH), BF16), pltpu.VMEM((SHORT_DEV, HK * DH), BF16),
+            pltpu.SemaphoreType.DMA((steps, 2)), pltpu.SemaphoreType.DMA((steps, 4)),
+            pltpu.SemaphoreType.DMA((2, 4))],
         compiler_params=pltpu.CompilerParams(vmem_limit_bytes=60 << 20),
         name="place_outputs",
-    )(back_a.reshape(GROUPS, N_DEV // GROUPS, ROWS_B, DH),
-      back_b.reshape(GROUPS, N_DEV // GROUPS, ROWS_A, DH), *short))
+    )(*results))
 
 
 def solution(mesh):

time: 168 us -> 167 us (level)
  no operation moved by 1% of the time
where the time goes in v3:
time: 167 us; the launch traced here: 165 us
  Pallas kernels  164 us (98%)
    pallas_call x1, Pallas kernels, per_device(): pl.pallas_call(kernel, out_shape=[shape(N_DEV, ROWS_B, DH), shape(N_DEV,...  159 us
    pallas_call x1, Pallas kernels, per_device(): pl.pallas_call(place, out_shape=[shape(ROWS, HQ * DH), shape(ROWS, HQ * D...  5.73 us

profile of v3, /device:TPU:1, one launch (start us, length us, event | category | flops | bytes accessed | tf_op | source)
XLA Modules:
  0.0 165.1 jit_solution(5509222332669085788)
XLA Ops:
  0.6 158.5 %relay_and_attend.1 = (bf16[128,72,128]{2,1,0:T(8,128)(2,1)}, bf16[128,112,128]{2,1,0:T(8,128)(2,1)}, bf16[128,2048]{1,0:T(8,128)(2,1)}, bf16[128,2048]{1,0:T(8,...) custom-call(s32[1,4]{1,0:T(1,128)} %lengths_ref.1, s32[64]{0:T(128)} %doc_len_ref.1, s32[64]{0:T(128)} %doc_group_ref.1, ...), custom_call_target="tpu_custom_call" | custom-call | tf_op jit(solution)/shard_map/relay_and_attend/pallas_call | solution.py:451
  159.2 5.7 %place_outputs.1 = (bf16[704,2048]{1,0:T(8,128)(2,1)}, bf16[704,2048]{1,0:T(8,128)(2,1)}, bf16[704,512]{1,0:T(8,128)(2,1)}, bf16[704,512]{1,0:T(8,128)(2,1)}) custom-call(bf16[128,72,128]{2,1,0:T(8,128)(2,1)} %get-tuple-element.10.back_a, bf16[128,112,128]{2,1,0:T(8,128)(2,1)} %get-tuple-element.11.back_b, bf16[128,2048]{1,0:T(8,128)(2,1)} %get-tuple-element.12.so_ref, ...), custom_call_target="tpu_custom_call" | custom-call | tf_op jit(solution)/shard_map/place_outputs/pallas_call | solution.py:482
